TPU v7x, 32 devices: a whole 2x2x4 slice. The times are simulated.
32 devices in a mesh: sect: 4 (over y, x), node: 8 (over z, core).
Axes of the slice: x: 2, y: 2, z: 4, core: 2. Of those that a mesh axis runs over, the one named last changes fastest.
Arguments:
- grid_feat: bfloat16 [8192, 512], P(('sect', 'node')), may hold values from -6 to 6
- edge_len: float32 [8192, 2], P(('sect', 'node')), may hold values from 0.2 to 1.5
- g2m_owner: int32 [8192, 2], P(('sect', 'node')), may hold values from 0 to 7, all different within a row; in each aligned block of 256 rows (0 to 255, 256 to 511, ...) at most 128 rows name the same one
- g2m_dst: int32 [8192, 2], P(('sect', 'node')), may hold values from 0 to 511
- enc_weight: bfloat16 [512, 512], replicated, may hold values from -0.25 to 0.25
- enc_vec: float32 [512], replicated, may hold values from -5 to 5
- mesh_init: bfloat16 [8, 512, 512], P('node', 'sect'), may hold values from -1.11 to 1.11
- mesh_weight: bfloat16 [512, 512], replicated, may hold values from -0.015625 to 0.015625
- halo_send: int32 [4, 8, 4, 8, 2], P('sect', 'node'), may hold values from 0 to 127
- mesh_src: int32 [8, 512, 8], P('node', 'sect'), may hold values from 0 to 191
- proc_weight: bfloat16 [2, 4, 512, 512], replicated, may hold values from -0.25 to 0.25
- cot: bfloat16 [8, 512, 512], P('node', 'sect'), may hold values from -16 to 16
Outputs:
- mesh_out: bfloat16 [8, 512, 512], P('node', 'sect')
- grid_grad: bfloat16 [8192, 512], P(('sect', 'node'))
Inputs may be any that keep to these rules, and one draw needn't show every extreme that they name: `g2m_owner`: within the 256 grid nodes of one device (aligned blocks), at most 128 edges name one mesh block, and some block is named by exactly 128 edges in some or all devices; the 2 edges of one grid node name different blocks. `mesh_src`: entries below 128 name own rows of the table, the others received rows.
All inputs are finite; a program needn't handle non-finite values.
Results may differ from a plain program's by a relative error of at most 0.009.
Values may be sent and summed in bfloat16 or wider, within the bound.
No kernel may reach another device: no remote copies, remote signals or barrier semaphores. Data moves between devices by JAX's collectives and lax.ppermute only.
A program may use at most 64 MiB of HBM per device.

v0:
```python
import functools
import math

import jax
import jax.numpy as jnp
from jax import lax
from jax.experimental import pallas as pl
from jax.experimental.pallas import tpu as pltpu
from jax.sharding import PartitionSpec as P

F32 = jnp.float32
BF16 = jnp.bfloat16
LANES = 128
META_ROWS = 16
MIB = 1024 * 1024


def sigmoid(value):
    return 0.5 * jnp.tanh(0.5 * value) + 0.5


def silu(value):
    return value * sigmoid(value)


def slope(value):
    sig = sigmoid(value)
    return sig * (1.0 + value * (1.0 - sig))


def dot(left, right):
    return jnp.dot(left, right, preferred_element_type=F32)


def dot_t(left, right):
    return lax.dot_general(left, right, (((1,), (1,)), ((), ())), preferred_element_type=F32)


def halves(value):
    high = value.astype(BF16)
    return high, (value - high.astype(F32)).astype(BF16)


def back_dot(grad, weight):
    rows = grad.shape[0]
    both = dot_t(jnp.concatenate(halves(grad), axis=0), weight)
    return both[:rows] + both[rows:]


def mark(equal):
    return jnp.where(equal, 1.0, 0.0).astype(BF16)


def iota(shape, axis):
    return lax.broadcasted_iota(jnp.int32, shape, axis)


def norm_parts(mixed):
    mean = jnp.mean(mixed, axis=-1, keepdims=True)
    centred = mixed - mean
    scale = lax.rsqrt(jnp.mean(centred * centred, axis=-1, keepdims=True) + 1e-05)
    return centred * scale, scale


def norm_back(grad, normed, scale):
    pull = grad * slope(normed)
    return scale * (
        pull
        - jnp.mean(pull, axis=-1, keepdims=True)
        - normed * jnp.mean(pull * normed, axis=-1, keepdims=True)
    )


def pack_kernel(block, feat, lens, owner, dst, out, held, own_held, dst_held, sems):
    rows = feat.shape[0]
    pairs = ((lens, held), (owner, own_held), (dst, dst_held), (feat, out.at[:rows, :]))
    copies = [
        pltpu.make_async_copy(source, target, sems.at[i])
        for i, (source, target) in enumerate(pairs)
    ]
    for copy in copies:
        copy.start()
    for copy in copies[:3]:
        copy.wait()
    high, middle = halves(held[...])
    low = (held[...] - high.astype(F32) - middle.astype(F32)).astype(BF16)
    far = dst_held[...]
    section = far // block
    found = [v.astype(F32) for v in (high, middle, low)]
    found += [v.astype(F32) for v in (own_held[...], section, far - section * block)]
    fill = META_ROWS - 6 * lens.shape[0]
    found.append(jnp.zeros((fill, rows), F32))
    meta = jnp.concatenate(found, axis=0).astype(BF16)
    out[rows:, :] = jnp.concatenate(
        [meta, jnp.zeros((META_ROWS, feat.shape[1] - rows), BF16)], axis=1
    )
    copies[3].wait()


def index_kernel(block, parts, sends, src_row, pick, pick_t, source, source_t):
    sects, count, nodes = sends.shape
    pieces = pick.shape[0]
    at = iota((1, pieces), 1)
    part, row = at % parts, at // parts
    peer = row // count
    whose = mark(iota((nodes, pieces), 0) == peer % nodes)
    place = jnp.zeros((1, pieces), F32)
    for t in range(sects):
        found = dot(sends[t].astype(F32).astype(BF16), whose)
        for c in range(count):
            here = jnp.logical_and(peer // nodes == t, row % count == c)
            place = place + jnp.where(here, found[c : c + 1], 0.0)
    place = place + (part * block).astype(F32)
    pick_t[...] = mark(iota((parts * block, pieces), 0) == place.astype(jnp.int32))
    turned = jnp.broadcast_to(place, (8, pieces)).T[:, :1].astype(jnp.int32)
    pick[...] = mark(iota((pieces, parts * block), 1) == turned)
    table_len = source_t.shape[0]
    column = src_row[...].astype(F32).T.astype(jnp.int32)
    ids = iota((block, 2 * table_len), 1)
    ids = jnp.where(ids >= table_len, ids - table_len, ids)
    ids_t = iota((table_len, block), 0)
    for k in range(src_row.shape[0]):
        rows = slice(k * block, (k + 1) * block)
        source[rows, :] = mark(ids == column[:, k : k + 1])
        source_t[:, rows] = mark(ids_t == src_row[k : k + 1, :])


def edge_data(feat, rows):
    return feat[rows:, :rows].astype(F32)


def edge_length(meta, fanout, k):
    high, middle, low = (meta[:, t * fanout + k : t * fanout + k + 1] for t in range(3))
    return high + middle + low


def spot_of(pick, fanout, k, section, node, nodes, block):
    owner, where, place = (pick((3 + t) * fanout + k).astype(jnp.int32) for t in range(3))
    apart = jnp.bitwise_xor(owner, node)
    order = lax.shift_right_logical(apart, 1) + jnp.bitwise_and(apart, 1) * (nodes // 2)
    return jnp.where(where == section, order * block + place, -1)


def encode_kernel(count, nodes, block, fanout, rows, last, who, *refs):
    feats = refs[:count]
    weight, vec = refs[count : count + 2]
    if last:
        before, keep, cross, message, spots = refs[count + 2 :]
    else:
        total, message, spots = refs[count + 2 :]
    section, node = who[0], who[1]
    for j in range(count):
        pre = dot(feats[j][:rows, :], weight[...])
        meta = edge_data(feats[j], rows)
        turned = meta.T
        for k in range(fanout):
            at = (j * fanout + k) * rows
            act = pre + edge_length(turned, fanout, k) * vec[...]
            message[at : at + rows, :] = silu(act).astype(BF16)
            spots[:, at : at + rows] = spot_of(
                lambda t, meta=meta: meta[t : t + 1], fanout, k, section, node, nodes, block
            )
    half = nodes // 2 * block
    step = min(half, 512)
    for out, base in ((cross, half), (keep, 0)) if last else ((total, 0),):

        def chunk(c, carry, out=out, base=base):
            start = pl.multiple_of(c * step, step)
            ids = iota((step, spots.shape[1]), 0) + (base + start)
            part = dot(mark(ids == spots[...]), message[...])
            if last:
                part = part + before[pl.ds(base + start, step), :]
            out[pl.ds(start, step), :] = part.astype(out.dtype)
            return carry

        lax.fori_loop(0, out.shape[0] // step, chunk, 0)


def slope_kernel(sects, fanout, rows, *refs):
    feats = refs[:sects]
    weight, vec = refs[sects : sects + 2]
    outs = refs[sects + 2 :]
    for j in range(sects):
        pre = dot(feats[j][:rows, :], weight[...])
        turned = edge_data(feats[j], rows).T
        for k in range(fanout):
            act = pre + edge_length(turned, fanout, k) * vec[...]
            outs[j][k * rows : (k + 1) * rows, :] = slope(act).astype(BF16)


def halo_rows(state, pick, parts):
    stacked = jnp.concatenate(
        [state[:, i * LANES : (i + 1) * LANES] for i in range(parts)], axis=0
    )
    return dot(pick, stacked).astype(BF16)


def join_pieces(pieces, parts):
    count = pieces.shape[0]
    shape = (count // parts, count)
    return jnp.concatenate(
        [
            dot(mark(iota(shape, 1) == iota(shape, 0) * parts + i), pieces).astype(BF16)
            for i in range(parts)
        ],
        axis=1,
    )


def cut_pieces(rows, parts):
    count = rows.shape[0]
    shape = (count * parts, count)
    total = None
    for i in range(parts):
        onehot = mark(iota(shape, 0) == iota(shape, 1) * parts + i)
        piece = dot(onehot, rows[:, i * LANES : (i + 1) * LANES])
        total = piece if total is None else total + piece
    return total.astype(BF16)


def add_pieces(pieces, pick_t, block, parts):
    total = dot(pick_t, pieces)
    return jnp.concatenate([total[i * block : (i + 1) * block] for i in range(parts)], axis=1)


def start_kernel(parts, sums, *refs):
    received, (init, weight, pick, state, mesh_pre, halo) = refs[:-6], refs[-6:]
    agg = sums[...]
    for ref in received:
        agg = agg + ref[...].astype(F32)
    pre = dot(agg.astype(BF16), weight[...])
    mesh_pre[...] = pre
    new = (init[...].astype(F32) + silu(pre)).astype(BF16)
    state[...] = new
    halo[...] = halo_rows(new, pick[...], parts)


def layer_forward(state, pieces, source, weights, parts):
    block = state.shape[0]
    halo = join_pieces(pieces, parts)
    table = jnp.concatenate([state, halo], axis=0)
    from_src = dot(table, weights(0))
    to_dst = dot(state, weights(1))
    gathered = dot(source[...], jnp.concatenate(halves(from_src), axis=0))
    agg = jnp.zeros(state.shape, F32)
    slopes = []
    for k in range(source.shape[0] // block):
        joined = gathered[k * block : (k + 1) * block] + to_dst
        sig = sigmoid(joined)
        act = joined * sig
        agg = agg + act
        slopes.append((sig + act * (1.0 - sig)).astype(BF16))
    mixed = dot(state, weights(2)) + dot(agg.astype(BF16), weights(3))
    return mixed, slopes


def layer_back(grad, mixed, slopes, source_t, weights):
    block = grad.shape[0]
    normed, scale = norm_parts(mixed)
    grad_mixed = norm_back(grad, normed, scale)
    grad_state = grad + back_dot(grad_mixed, weights(2))
    grad_agg = back_dot(grad_mixed, weights(3))
    total = jnp.zeros(grad.shape, F32)
    highs, lows = [], []
    for found in slopes:
        piece = grad_agg * found.astype(F32)
        total = total + piece
        high, low = halves(piece)
        highs.append(high)
        lows.append(low)
    onehot = source_t[...]
    grad_src = dot(onehot, jnp.concatenate(highs, axis=0)) + dot(
        onehot, jnp.concatenate(lows, axis=0)
    )
    grad_state = grad_state + back_dot(total, weights(1))
    grad_table = back_dot(grad_src, weights(0))
    return grad_state + grad_table[:block], grad_table[block:]


def layer_weights(weights, layer):
    return lambda i: weights[layer, i]


def first_kernel(
    layer, parts, state, pieces, source, weights, pick, new, mixed, slopes, halo
):
    block = state.shape[0]
    own = state[...]
    used = layer_weights(weights, layer)
    value, found = layer_forward(own, pieces[...], source, used, parts)
    mixed[...] = value
    for k, part in enumerate(found):
        slopes[k * block : (k + 1) * block, :] = part
    normed, _ = norm_parts(value)
    result = (own.astype(F32) + silu(normed)).astype(BF16)
    new[...] = result
    halo[...] = halo_rows(result, pick[...], parts)


def last_kernel(
    layer, parts, state, pieces, source, source_t, weights, cot, out, grad_own, grad_halo
):
    own = state[...]
    used = layer_weights(weights, layer)
    value, found = layer_forward(own, pieces[...], source, used, parts)
    normed, _ = norm_parts(value)
    out[...] = (own.astype(F32) + silu(normed)).astype(BF16)
    mine, sent = layer_back(cot[...].astype(F32), value, found, source_t, used)
    grad_own[...] = mine
    grad_halo[...] = cut_pieces(sent.astype(BF16), parts)


def back_kernel(
    layer,
    parts,
    mine,
    returned,
    pick_t,
    mixed,
    slopes,
    source_t,
    weights,
    grad_own,
    grad_halo,
):
    block = mine.shape[0]
    grad = mine[...] + add_pieces(returned[...], pick_t[...], block, parts)
    fan = slopes.shape[0] // block
    found = [slopes[k * block : (k + 1) * block, :] for k in range(fan)]
    used = layer_weights(weights, layer)
    own, sent = layer_back(grad, mixed[...], found, source_t, used)
    grad_own[...] = own
    grad_halo[...] = cut_pieces(sent.astype(BF16), parts)


def mesh_back_kernel(parts, mine, returned, pick_t, mesh_pre, weight, out):
    block = mine.shape[0]
    grad = mine[...] + add_pieces(returned[...], pick_t[...], block, parts)
    out[...] = back_dot(grad * slope(mesh_pre[...]), weight[...]).astype(BF16)


def message_back_kernel(nodes, block, fanout, count, who, *refs):
    feats, slopes = refs[:count], refs[count : 2 * count]
    grads, outs = refs[2 * count : -count], refs[-count:]
    rows = outs[0].shape[0]
    ids = iota((rows, nodes * block), 1)
    marks = []
    for feat in feats:
        turned = edge_data(feat, rows).T
        for k in range(fanout):
            spot = spot_of(
                lambda t, turned=turned: turned[:, t : t + 1],
                fanout,
                k,
                who[0],
                who[1],
                nodes,
                block,
            )
            marks.append(mark(ids == spot))
    picked = dot(
        jnp.concatenate(marks, axis=0), jnp.concatenate([ref[...] for ref in grads], axis=0)
    )
    for j, out in enumerate(outs):
        total = jnp.zeros(out.shape, F32)
        for k in range(fanout):
            at = (j * fanout + k) * rows
            part = slopes[j][k * rows : (k + 1) * rows, :].astype(F32)
            total = total + picked[at : at + rows] * part
        out[...] = total.astype(out.dtype)


def grid_back_kernel(*refs):
    *parts, weight, out = refs
    total = parts[0][...].astype(F32)
    for ref in parts[1:]:
        total = total + ref[...].astype(F32)
    out[...] = back_dot(total, weight[...]).astype(BF16)


def call(kernel, outs, args, smem=0, scratch=(), macs=0, scalars=0, space=pltpu.VMEM):
    specs = [pl.BlockSpec(memory_space=pltpu.SMEM)] * smem
    specs += [pl.BlockSpec(memory_space=space)] * (len(args) - smem)
    moved = sum(a.size * a.dtype.itemsize for a in list(args) + list(outs))
    held = sum(math.prod(a.shape) * 4 for a in scratch)
    limit = 2 * (moved + held) + 6 * MIB
    result = pl.pallas_call(
        kernel,
        out_shape=list(outs),
        in_specs=specs,
        out_specs=[pl.BlockSpec(memory_space=pltpu.VMEM)] * len(outs),
        scratch_shapes=list(scratch),
        compiler_params=pltpu.CompilerParams(vmem_limit_bytes=limit),
        cost_estimate=pl.CostEstimate(
            flops=2 * macs, bytes_accessed=moved, transcendentals=scalars
        ),
    )(*args)
    return result


def shape(dims, dtype):
    return jax.ShapeDtypeStruct(dims, dtype)


def swap(value, axis, apart):
    size = lax.axis_size(axis)
    return lax.ppermute(value, axis, [(i, i ^ apart) for i in range(size)])


def body(
    grid_feat,
    edge_len,
    g2m_owner,
    g2m_dst,
    enc_weight,
    enc_vec,
    mesh_init,
    mesh_weight,
    halo_send,
    mesh_src,
    proc_weight,
    cot,
):
    nodes = lax.axis_size("node")
    sects = lax.axis_size("sect")
    width = grid_feat.shape[1]
    grid_rows, fanout = edge_len.shape
    block = mesh_init.shape[1]
    parts = width // LANES
    both = ("sect", "node")
    who = jnp.stack([lax.axis_index("sect"), lax.axis_index("node")]).astype(jnp.int32)

    ends = pltpu.VMEM((fanout, grid_rows), jnp.int32)
    (packed,) = call(
        functools.partial(pack_kernel, block),
        [shape((grid_rows + META_ROWS, width), BF16)],
        [
            pltpu.with_memory_space_constraint(value, pltpu.HBM)
            for value in (grid_feat, edge_len.T, g2m_owner.T, g2m_dst.T)
        ],
        scratch=[
            pltpu.VMEM((fanout, grid_rows), F32),
            ends,
            ends,
            pltpu.SemaphoreType.DMA((4,)),
        ],
        space=pltpu.HBM,
    )
    feats = [packed] + [swap(packed, "sect", j) for j in range(1, sects)]
    vec = enc_vec[None, :]
    half = nodes // 2

    def encode(used, last, outs, extra):
        edges = len(used) * grid_rows * fanout
        return call(
            functools.partial(
                encode_kernel, len(used), nodes, block, fanout, grid_rows, last
            ),
            outs,
            [who, *used, enc_weight, vec, *extra],
            smem=1,
            scratch=[pltpu.VMEM((edges, width), BF16), pltpu.VMEM((1, edges), jnp.int32)],
            macs=len(used) * grid_rows * width * width + edges * nodes * block * width,
            scalars=edges * width,
        )

    before = encode(feats[:1], False, [shape((nodes * block, width), F32)], [])
    sends = halo_send[0, 0].transpose(0, 2, 1)
    src_row = mesh_src[0].T
    fan = src_row.shape[0]
    pieces = halo_send[0, 0].size * parts
    table_len = block + halo_send[0, 0].size
    found = call(
        functools.partial(index_kernel, block, parts),
        [
            shape((pieces, parts * block), BF16),
            shape((parts * block, pieces), BF16),
            shape((fan * block, 2 * table_len), BF16),
            shape((table_len, fan * block), BF16),
        ],
        [sends, src_row],
        scalars=4 * fan * block * table_len,
    )
    *before, pick, pick_t, source, source_t = lax.optimization_barrier((*before, *found))
    keep, cross = encode(
        feats[1:], True, [shape((half * block, width), BF16)] * 2, before
    )

    pair = keep.astype(F32) + swap(cross, "node", 1).astype(F32)
    pair = pair.reshape(half, block, width)
    arrived = [swap(pair[q].astype(BF16), "node", 2 * q) for q in range(1, half)]

    slopes = call(
        functools.partial(slope_kernel, sects, fanout, grid_rows),
        [shape((fanout * grid_rows, width), BF16)] * sects,
        [*feats, enc_weight, vec],
        macs=sects * grid_rows * width * width,
        scalars=sects * grid_rows * fanout * width,
    )
    tied = lax.optimization_barrier((*arrived, *slopes))
    arrived, slopes = tied[: half - 1], tied[half - 1 :]

    halo_shape = shape((pieces, LANES), BF16)
    row_low, row_high = shape((block, width), BF16), shape((block, width), F32)

    def exchange(value):
        return lax.all_to_all(value, both, split_axis=0, concat_axis=0, tiled=True)

    state, mesh_pre, halo = call(
        functools.partial(start_kernel, parts),
        [row_low, row_high, halo_shape],
        [pair[0], *arrived, mesh_init[0], mesh_weight, pick],
        macs=block * width * width,
        scalars=block * width,
    )
    layer_macs = 6 * block * width * width + 2 * fan * block * 2 * block * width
    assert proc_weight.shape[0] == 2
    state, mixed, slope_first, halo = call(
        functools.partial(first_kernel, 0, parts),
        [row_low, row_high, shape((fan * block, width), BF16), halo_shape],
        [state, exchange(halo), source, proc_weight, pick],
        macs=layer_macs,
        scalars=fan * block * width,
    )
    mesh_out, grad, halo = call(
        functools.partial(last_kernel, 1, parts),
        [row_low, row_high, halo_shape],
        [state, exchange(halo), source, source_t, proc_weight, cot[0]],
        macs=3 * layer_macs,
        scalars=fan * block * width,
    )
    grad, halo = call(
        functools.partial(back_kernel, 0, parts),
        [row_high, halo_shape],
        [grad, exchange(halo), pick_t, mixed, slope_first, source_t, proc_weight],
        macs=2 * layer_macs,
        scalars=block * width,
    )
    (grad_sum,) = call(
        functools.partial(mesh_back_kernel, parts),
        [row_low],
        [grad, exchange(halo), pick_t, mesh_pre, mesh_weight],
        macs=2 * block * width * width,
        scalars=block * width,
    )

    same = [grad_sum] + [swap(grad_sum, "node", 2 * q) for q in range(1, half)]
    other = [swap(rows, "node", 1) for rows in same]
    parts_of = {}
    for group in ([sects - 1], list(range(1, sects - 1)), [0]):
        found = call(
            functools.partial(message_back_kernel, nodes, block, fanout, len(group)),
            [shape((grid_rows, width), BF16)] * len(group),
            [who, *(feats[j] for j in group), *(slopes[j] for j in group), *same, *other],
            smem=1,
            macs=len(group) * fanout * grid_rows * nodes * block * width,
        )
        for j, grad_pre in zip(group, found):
            parts_of[j] = swap(grad_pre, "sect", j) if j else grad_pre
    mine, *sent = (parts_of[j] for j in range(sects))
    (grid_grad,) = call(
        grid_back_kernel,
        [shape((grid_rows, width), BF16)],
        [mine, *sent, enc_weight],
        macs=2 * grid_rows * width * width,
    )
    return (mesh_out[None], grid_grad)


def solution(mesh):
    return jax.shard_map(
        body,
        mesh=mesh,
        in_specs=(
            P(("sect", "node"), None),
            P(("sect", "node"), None),
            P(("sect", "node"), None),
            P(("sect", "node"), None),
            P(),
            P(),
            P("node", "sect", None),
            P(),
            P("sect", "node", None, None, None),
            P("node", "sect", None),
            P(),
            P("node", "sect", None),
        ),
        out_specs=(P("node", "sect", None), P(("sect", "node"), None)),
        check_vma=False,
    )
```

profile of v0, /device:TPU:0, one launch (start us, length us, event | category | flops | bytes accessed | tf_op | source)
XLA Modules:
  0.0 120.7 jit_solution(12108161772141772554)
XLA Ops:
  0.6 0.0 copy-start.3
  0.6 0.0 copy-start.6
  0.7 1.1 shard_map.131.refs_0_
  1.8 4.0 %collective-permute-start.2 = (bf16[272,512]{1,0:T(8,128)(2,1)S(1)}, bf16[272,512]{1,0:T(8,128)(2,1)S(1)}, u32[]{:S(2)}, u32[]{:S(2)}) collective-permute-start(bf16[272,512]{1,0:T(8,128)(2,1)S(1)} %shard_map.131.refs_0_), channel_id=1, source_target_pairs={{0,24},{8,16},{16,8},{24,0},{1,25},{9,17},{17,9},{25,1},{2,26},{10... | collective-permute-start | bytes 835592 | tf_op jit(solution)/shard_map/ppermute | solution.py:407
  5.7 0.5 collective-permute-start.1
  6.2 0.1 collective-permute-start
  6.4 0.7 copy-done.8
  7.0 0.7 copy-done.9
  7.7 0.7 shard_map.133
  8.4 0.1 pad_add_fusion.who
  8.5 1.0 copy-done.2
  9.5 0.7 copy-done.5
  10.2 1.9 %shard_map.132.refs_5_ = f32[1024,512]{1,0:T(8,128)S(1)} custom-call(s32[2]{0:T(128)S(1)} %pad_add_fusion.who, bf16[272,512]{1,0:T(8,128)(2,1)S(1)} %shard_map.131.refs_0_, bf16[512,512]{1,0:T(8,128)(2,1)S(1)} %copy-done.2, f32[1,512]{1,0:T(1,128)S(1)} %bitcast.32), custom_call_target="tpu_custom_call" | custom-call | flops 671088640 | bytes 2902024 | tf_op jit(solution)/shard_map/pallas_call | solution.py:387
  12.1 1.1 collective-permute-done.2.refs_2_.refs_3_.refs_0_
  13.2 5.1 %collective-permute-done.1.refs_1_.refs_2_ = bf16[272,512]{1,0:T(8,128)(2,1)S(1)} collective-permute-done((bf16[272,512]{1,0:T(8,128)(2,1)S(1)}, bf16[272,512]{1,0:T(8,128)(2,1)S(1)}, u32[]{:S(2)}, u32[]{:S(2)}) %collective-permute-start.1) | collective-permute-done | bytes 278560 | tf_op jit(solution)/shard_map/ppermute | solution.py:407
  18.3 0.3 collective-permute-done.refs_0_.refs_1_
  18.6 3.2 %shard_map.134 = (bf16[512,512]{1,0:T(8,128)(2,1)S(1)}, bf16[512,512]{1,0:T(8,128)(2,1)S(1)}) custom-call(s32[2]{0:T(128)S(1)} %pad_add_fusion.who, bf16[272,512]{1,0:T(8,128)(2,1)S(1)} %collective-permute-done.refs_0_.refs_1_, bf16[272,512]{1,0:T(8,128)(2,1)S(1)} %collective-permute-done.1.refs_1_.refs_2_, ...), custom_call_target="tpu_custom_call" | custom-call | flops 2013265920 | bytes 4507656 | tf_op jit(solution)/shard_map/pallas_call | solution.py:387
  21.8 0.0 copy-start.1
  21.8 0.0 copy-start.4
  21.8 0.0 copy-start
  21.9 0.1 collective-permute-start.3
  21.9 1.9 %collective-permute-done.3 = bf16[512,512]{1,0:T(8,128)(2,1)S(1)} collective-permute-done((bf16[512,512]{1,0:T(8,128)(2,1)S(1)}, bf16[512,512]{1,0:T(8,128)(2,1)S(1)}, u32[]{:S(2)}, u32[]{:S(2)}) %collective-permute-start.3) | collective-permute-done | bytes 524320 | tf_op jit(solution)/shard_map/ppermute | solution.py:407
  23.8 0.2 fusion
  24.1 3.7 %collective-permute-start.6 = (bf16[128,512]{1,0:T(8,128)(2,1)S(1)}, bf16[128,512]{1,0:T(8,128)(2,1)S(1)}, u32[]{:S(2)}, u32[]{:S(2)}) collective-permute-start(bf16[128,512]{1,0:T(8,128)(2,1)S(1)} %get-tuple-element.76), channel_id=1, source_target_pairs={{0,6},{1,7},{2,4},{3,5},{4,2},{5,3},{6,0},{7,1},{8,14},{9,15},{10,... | collective-permute-start | bytes 393224 | tf_op jit(solution)/shard_map/ppermute | solution.py:407
  27.7 0.0 collective-permute-start.5
  27.7 0.8 collective-permute-start.4
  28.5 2.0 %shard_map.135 = (bf16[512,512]{1,0:T(8,128)(2,1)S(1)}, bf16[512,512]{1,0:T(8,128)(2,1)S(1)}, bf16[512,512]{1,0:T(8,128)(2,1)S(1)}, bf16[512,512]{1,0:T(8,128)(2,1)S(1)}) custom-call(bf16[272,512]{1,0:T(8,128)(2,1)S(1)} %shard_map.131.refs_0_, bf16[272,512]{1,0:T(8,128)(2,1)S(1)} %collective-permute-done.refs_0_.refs_1_, ...), custom_call_target="tpu_custom_call" | custom-call | flops 536870912 | bytes 3737600 | tf_op jit(solution)/shard_map/pallas_call | solution.py:387
  30.5 0.0 copy-start.7
  30.5 1.8 %collective-permute-done.6.refs_2_ = bf16[128,512]{1,0:T(8,128)(2,1)S(1)} collective-permute-done((bf16[128,512]{1,0:T(8,128)(2,1)S(1)}, bf16[128,512]{1,0:T(8,128)(2,1)S(1)}, u32[]{:S(2)}, u32[]{:S(2)}) %collective-permute-start.6) | collective-permute-done | bytes 131104 | tf_op jit(solution)/shard_map/ppermute | solution.py:407
  32.4 6.7 %collective-permute-done.5.refs_1_ = bf16[128,512]{1,0:T(8,128)(2,1)S(1)} collective-permute-done((bf16[128,512]{1,0:T(8,128)(2,1)S(1)}, bf16[128,512]{1,0:T(8,128)(2,1)S(1)}, u32[]{:S(2)}, u32[]{:S(2)}) %collective-permute-start.5) | collective-permute-done | bytes 131104 | tf_op jit(solution)/shard_map/ppermute | solution.py:407
  39.1 0.0 collective-permute-done.4.refs_0_
  39.1 0.5 shard_map.136
  39.6 11.2 %all_to_all.44 = bf16[32,8,128]{2,1,0:T(8,128)(2,1)S(1)} all-to-all(bf16[32,8,128]{2,1,0:T(8,128)(2,1)S(1)} %bitcast.27), channel_id=1, replica_groups=mesh['sect'=4,'node'=8] {'sect','node'}, dimensions={0} | all-to-all | bytes 131072 | tf_op jit(solution)/shard_map/all_to_all | solution.py:507
  50.8 2.2 %shard_map.137 = (bf16[128,512]{1,0:T(8,128)(2,1)S(1)}, f32[128,512]{1,0:T(8,128)S(1)}, bf16[1024,512]{1,0:T(8,128)(2,1)S(1)}, bf16[256,128]{1,0:T(8,128)(2,1)S(1)}) custom-call(bf16[128,512]{1,0:T(8,128)(2,1)S(1)} %get-tuple-element.53.state, bf16[256,128]{1,0:T(8,128)(2,1)S(1)} %bitcast.23, bf16[1024,384]{1,0:T(8,128)(2,1)S(1)} %get-tuple-element.55.source, ...), custom_call_target="tpu_custom_call" | custom-call | flops 939524096 | bytes 6946816 | tf_op jit(solution)/shard_map/pallas_call | solution.py:387
  53.0 9.1 %all_to_all.45 = bf16[32,8,128]{2,1,0:T(8,128)(2,1)S(1)} all-to-all(bf16[32,8,128]{2,1,0:T(8,128)(2,1)S(1)} %bitcast.28), channel_id=1, replica_groups=mesh['sect'=4,'node'=8] {'sect','node'}, dimensions={0} | all-to-all | bytes 131072 | tf_op jit(solution)/shard_map/all_to_all | solution.py:507
  62.0 4.3 %shard_map.138 = (bf16[128,512]{1,0:T(8,128)(2,1)}, f32[128,512]{1,0:T(8,128)S(1)}, bf16[256,128]{1,0:T(8,128)(2,1)S(1)}) custom-call(bf16[128,512]{1,0:T(8,128)(2,1)S(1)} %get-tuple-element.56.state, bf16[256,128]{1,0:T(8,128)(2,1)S(1)} %bitcast.30, bf16[1024,384]{1,0:T(8,128)(2,1)S(1)} %get-tuple-element.55.source, ...), custom_call_target="tpu_custom_call" | custom-call | flops 2818572288 | bytes 6160384 | tf_op jit(solution)/shard_map/pallas_call | solution.py:387
  66.3 9.1 %all_to_all.46 = bf16[32,8,128]{2,1,0:T(8,128)(2,1)S(1)} all-to-all(bf16[32,8,128]{2,1,0:T(8,128)(2,1)S(1)} %bitcast.31), channel_id=1, replica_groups=mesh['sect'=4,'node'=8] {'sect','node'}, dimensions={0} | all-to-all | bytes 131072 | tf_op jit(solution)/shard_map/all_to_all | solution.py:507
  75.4 2.2 %shard_map.139 = (f32[128,512]{1,0:T(8,128)S(1)}, bf16[256,128]{1,0:T(8,128)(2,1)S(1)}) custom-call(f32[128,512]{1,0:T(8,128)S(1)} %get-tuple-element.61.mine, bf16[256,128]{1,0:T(8,128)(2,1)S(1)} %bitcast.26, bf16[512,256]{1,0:T(8,128)(2,1)S(1)} %get-tuple-element.63.pick_t, f32[128,512]{1,0:T(8,128)S(1)} %get-tuple-element.64.mixed, ...), custom_call_target="tpu_custom_call" | custom-call | flops 1879048192 | bytes 6815744 | tf_op jit(solution)/shard_map/pallas_call | solution.py:387
  77.6 9.1 %all_to_all.47 = bf16[32,8,128]{2,1,0:T(8,128)(2,1)S(1)} all-to-all(bf16[32,8,128]{2,1,0:T(8,128)(2,1)S(1)} %bitcast.29), channel_id=1, replica_groups=mesh['sect'=4,'node'=8] {'sect','node'}, dimensions={0} | all-to-all | bytes 131072 | tf_op jit(solution)/shard_map/all_to_all | solution.py:507
  86.6 0.5 shard_map.140.refs_2_.refs_4_
  87.1 0.8 collective-permute-start.9
  87.9 1.2 %collective-permute-start.8 = (bf16[128,512]{1,0:T(8,128)(2,1)S(1)}, bf16[128,512]{1,0:T(8,128)(2,1)S(1)}, u32[]{:S(2)}, u32[]{:S(2)}) collective-permute-start(bf16[128,512]{1,0:T(8,128)(2,1)S(1)} %shard_map.140.refs_2_.refs_4_), channel_id=1, source_target_pairs={{0,4},{1,5},{2,6},{3,7},{4,0},{5,1},{6,2},{7,3},{8,12},{9,13},{10,... | collective-permute-start | bytes 393224 | tf_op jit(solution)/shard_map/ppermute | solution.py:407
  89.1 2.5 %collective-permute-start.7 = (bf16[128,512]{1,0:T(8,128)(2,1)S(1)}, bf16[128,512]{1,0:T(8,128)(2,1)S(1)}, u32[]{:S(2)}, u32[]{:S(2)}) collective-permute-start(bf16[128,512]{1,0:T(8,128)(2,1)S(1)} %shard_map.140.refs_2_.refs_4_), channel_id=1, source_target_pairs={{0,2},{1,3},{2,0},{3,1},{4,6},{5,7},{6,4},{7,5},{8,10},{9,11},{10,... | collective-permute-start | bytes 393224 | tf_op jit(solution)/shard_map/ppermute | solution.py:407
  91.6 0.0 collective-permute-start.10
  91.6 3.9 %collective-permute-done.9.refs_5_.refs_7_ = bf16[128,512]{1,0:T(8,128)(2,1)S(1)} collective-permute-done((bf16[128,512]{1,0:T(8,128)(2,1)S(1)}, bf16[128,512]{1,0:T(8,128)(2,1)S(1)}, u32[]{:S(2)}, u32[]{:S(2)}) %collective-permute-start.9) | collective-permute-done | bytes 131104 | tf_op jit(solution)/shard_map/ppermute | solution.py:407
  95.5 0.0 collective-permute-start.13
  95.5 5.6 %collective-permute-done.8.refs_4_.refs_6_ = bf16[128,512]{1,0:T(8,128)(2,1)S(1)} collective-permute-done((bf16[128,512]{1,0:T(8,128)(2,1)S(1)}, bf16[128,512]{1,0:T(8,128)(2,1)S(1)}, u32[]{:S(2)}, u32[]{:S(2)}) %collective-permute-start.8) | collective-permute-done | bytes 131104 | tf_op jit(solution)/shard_map/ppermute | solution.py:407
  101.0 0.0 collective-permute-start.12
  101.1 0.0 collective-permute-done.7.refs_3_.refs_5_
  101.1 0.5 collective-permute-start.11
  101.6 0.0 collective-permute-done.10.refs_6_.refs_8_
  101.6 0.0 collective-permute-done.13.refs_9_.refs_11_
  101.6 0.8 collective-permute-done.12.refs_8_.refs_10_
  102.4 0.2 collective-permute-done.11.refs_7_.refs_9_
  102.6 2.4 %shard_map.142 = (bf16[256,512]{1,0:T(8,128)(2,1)S(1)}, bf16[256,512]{1,0:T(8,128)(2,1)S(1)}) custom-call(s32[2]{0:T(128)S(1)} %pad_add_fusion.who, bf16[272,512]{1,0:T(8,128)(2,1)S(1)} %collective-permute-done.refs_0_.refs_1_, bf16[272,512]{1,0:T(8,128)(2,1)S(1)} %collective-permute-done.1.refs_1_.refs_2_, bf16[512,512]{1,0:T(8,128)(2,1)S(1)} %get-tuple-element.69.refs_2_, ...), custom_call_target="tpu_custom_call" | custom-call | flops 1073741824 | bytes 3178504 | tf_op jit(solution)/shard_map/pallas_call | solution.py:387
  105.0 0.7 collective-permute-start.14
  105.6 0.5 collective-permute-start.15
  106.2 1.6 %shard_map.143 = bf16[256,512]{1,0:T(8,128)(2,1)S(1)} custom-call(s32[2]{0:T(128)S(1)} %pad_add_fusion.who, bf16[272,512]{1,0:T(8,128)(2,1)S(1)} %collective-permute-done.2.refs_2_.refs_3_.refs_0_, bf16[512,512]{1,0:T(8,128)(2,1)S(1)} %get-tuple-element.73.refs_1_, bf16[128,512]{1,0:T(8,128)(2,1)S(1)} %shard_map.140.refs_2_.refs_4_, ...), custom_call_target="tpu_custom_call" | custom-call | flops 536870912 | bytes 2113544 | tf_op jit(solution)/shard_map/pallas_call | solution.py:387
  107.9 2.4 %collective-permute-start.16 = (bf16[256,512]{1,0:T(8,128)(2,1)S(1)}, bf16[256,512]{1,0:T(8,128)(2,1)S(1)}, u32[]{:S(2)}, u32[]{:S(2)}) collective-permute-start(bf16[256,512]{1,0:T(8,128)(2,1)S(1)} %shard_map.143), channel_id=1, source_target_pairs={{0,24},{8,16},{16,8},{24,0},{1,25},{9,17},{17,9},{25,1},{2,26},{10... | collective-permute-start | bytes 786440 | tf_op jit(solution)/shard_map/ppermute | solution.py:407
  110.3 1.6 %shard_map.141.refs_0_ = bf16[256,512]{1,0:T(8,128)(2,1)S(1)} custom-call(s32[2]{0:T(128)S(1)} %pad_add_fusion.who, bf16[272,512]{1,0:T(8,128)(2,1)S(1)} %shard_map.131.refs_0_, bf16[512,512]{1,0:T(8,128)(2,1)S(1)} %get-tuple-element.60.refs_1_, bf16[128,512]{1,0:T(8,128)(2,1)S(1)} %shard_map.140.refs_2_.refs_4_, ...), custom_call_target="tpu_custom_call" | custom-call | flops 536870912 | bytes 2113544 | tf_op jit(solution)/shard_map/pallas_call | solution.py:387
  111.9 2.3 %collective-permute-done.14.refs_1_ = bf16[256,512]{1,0:T(8,128)(2,1)S(1)} collective-permute-done((bf16[256,512]{1,0:T(8,128)(2,1)S(1)}, bf16[256,512]{1,0:T(8,128)(2,1)S(1)}, u32[]{:S(2)}, u32[]{:S(2)}) %collective-permute-start.14) | collective-permute-done | bytes 262176 | tf_op jit(solution)/shard_map/ppermute | solution.py:407
  114.2 5.3 %collective-permute-done.15.refs_2_ = bf16[256,512]{1,0:T(8,128)(2,1)S(1)} collective-permute-done((bf16[256,512]{1,0:T(8,128)(2,1)S(1)}, bf16[256,512]{1,0:T(8,128)(2,1)S(1)}, u32[]{:S(2)}, u32[]{:S(2)}) %collective-permute-start.15) | collective-permute-done | bytes 262176 | tf_op jit(solution)/shard_map/ppermute | solution.py:407
  119.5 0.0 collective-permute-done.16.refs_3_
  119.5 1.2 shard_map.144
  (12 shorter events, 0.1 us)
Async XLA Ops:
  0.6 18.0 %copy-start.3 = (bf16[512,512]{1,0:T(8,128)(2,1)S(1)}, bf16[512,512]{1,0:T(8,128)(2,1)}, u32[]{:S(2)}) copy-start(bf16[512,512]{1,0:T(8,128)(2,1)} %refs_4_.5) | copy-start | bytes 1572868
  0.6 18.0 %copy-start.6 = (f32[512]{0:T(512)S(1)}, f32[512]{0:T(512)}, u32[]{:S(2)}) copy-start(f32[512]{0:T(512)} %param.17) | copy-start | bytes 6148
  1.8 11.5 %collective-permute-start.2 = (bf16[272,512]{1,0:T(8,128)(2,1)S(1)}, bf16[272,512]{1,0:T(8,128)(2,1)S(1)}, u32[]{:S(2)}, u32[]{:S(2)}) collective-permute-start(bf16[272,512]{1,0:T(8,128)(2,1)S(1)} %shard_map.131.refs_0_), channel_id=1, source_target_pairs={{0,24},{8,16},{16,8},{24,0},{1,25},{9,17},{17,9},{25,1},{2,26},{10... | collective-permute-start | bytes 835592 | tf_op jit(solution)/shard_map/ppermute | solution.py:407
  5.7 12.6 %collective-permute-start.1 = (bf16[272,512]{1,0:T(8,128)(2,1)S(1)}, bf16[272,512]{1,0:T(8,128)(2,1)S(1)}, u32[]{:S(2)}, u32[]{:S(2)}) collective-permute-start(bf16[272,512]{1,0:T(8,128)(2,1)S(1)} %shard_map.131.refs_0_), channel_id=1, source_target_pairs={{0,16},{8,24},{16,0},{24,8},{1,17},{9,25},{17,1},{25,9},{2,18},{10... | collective-permute-start | bytes 835592 | tf_op jit(solution)/shard_map/ppermute | solution.py:407
  6.2 12.4 %collective-permute-start = (bf16[272,512]{1,0:T(8,128)(2,1)S(1)}, bf16[272,512]{1,0:T(8,128)(2,1)S(1)}, u32[]{:S(2)}, u32[]{:S(2)}) collective-permute-start(bf16[272,512]{1,0:T(8,128)(2,1)S(1)} %shard_map.131.refs_0_), channel_id=1, source_target_pairs={{0,8},{8,0},{16,24},{24,16},{1,9},{9,1},{17,25},{25,17},{2,10},{10... | collective-permute-start | bytes 835592 | tf_op jit(solution)/shard_map/ppermute | solution.py:407
  6.4 0.7 copy-start.8
  7.0 0.7 copy-start.9
  8.5 1.0 copy-start.2
  9.5 0.7 copy-start.5
  21.8 17.3 %copy-start.1 = (bf16[512,512]{1,0:T(8,128)(2,1)S(1)}, bf16[512,512]{1,0:T(8,128)(2,1)}, u32[]{:S(2)}) copy-start(bf16[512,512]{1,0:T(8,128)(2,1)} %weight.1) | copy-start | bytes 1572868
  21.8 17.3 %copy-start.4 = (bf16[1,128,512]{2,1,0:T(8,128)(2,1)S(1)}, bf16[1,128,512]{2,1,0:T(8,128)(2,1)}, u32[]{:S(2)}) copy-start(bf16[1,128,512]{2,1,0:T(8,128)(2,1)} %param.18) | copy-start | bytes 393220
  21.8 28.9 %copy-start = (bf16[2,4,512,512]{3,2,1,0:T(8,128)(2,1)S(1)}, bf16[2,4,512,512]{3,2,1,0:T(8,128)(2,1)}, u32[]{:S(2)}) copy-start(bf16[2,4,512,512]{3,2,1,0:T(8,128)(2,1)} %weights.5) | copy-start | bytes 12582916
  21.9 2.0 %collective-permute-start.3 = (bf16[512,512]{1,0:T(8,128)(2,1)S(1)}, bf16[512,512]{1,0:T(8,128)(2,1)S(1)}, u32[]{:S(2)}, u32[]{:S(2)}) collective-permute-start(bf16[512,512]{1,0:T(8,128)(2,1)S(1)} %get-tuple-element.44), channel_id=1, source_target_pairs={{0,1},{1,0},{2,3},{3,2},{4,5},{5,4},{6,7},{7,6},{8,9},{9,8},{10,11... | collective-permute-start | bytes 1572872 | tf_op jit(solution)/shard_map/ppermute | solution.py:407
  24.1 8.3 %collective-permute-start.6 = (bf16[128,512]{1,0:T(8,128)(2,1)S(1)}, bf16[128,512]{1,0:T(8,128)(2,1)S(1)}, u32[]{:S(2)}, u32[]{:S(2)}) collective-permute-start(bf16[128,512]{1,0:T(8,128)(2,1)S(1)} %get-tuple-element.76), channel_id=1, source_target_pairs={{0,6},{1,7},{2,4},{3,5},{4,2},{5,3},{6,0},{7,1},{8,14},{9,15},{10,... | collective-permute-start | bytes 393224 | tf_op jit(solution)/shard_map/ppermute | solution.py:407
  27.7 11.4 %collective-permute-start.5 = (bf16[128,512]{1,0:T(8,128)(2,1)S(1)}, bf16[128,512]{1,0:T(8,128)(2,1)S(1)}, u32[]{:S(2)}, u32[]{:S(2)}) collective-permute-start(bf16[128,512]{1,0:T(8,128)(2,1)S(1)} %get-tuple-element.77), channel_id=1, source_target_pairs={{0,4},{1,5},{2,6},{3,7},{4,0},{5,1},{6,2},{7,3},{8,12},{9,13},{10,... | collective-permute-start | bytes 393224 | tf_op jit(solution)/shard_map/ppermute | solution.py:407
  27.7 11.4 %collective-permute-start.4 = (bf16[128,512]{1,0:T(8,128)(2,1)S(1)}, bf16[128,512]{1,0:T(8,128)(2,1)S(1)}, u32[]{:S(2)}, u32[]{:S(2)}) collective-permute-start(bf16[128,512]{1,0:T(8,128)(2,1)S(1)} %get-tuple-element.78), channel_id=1, source_target_pairs={{0,2},{1,3},{2,0},{3,1},{4,6},{5,7},{6,4},{7,5},{8,10},{9,11},{10,... | collective-permute-start | bytes 393224 | tf_op jit(solution)/shard_map/ppermute | solution.py:407
  30.5 31.5 %copy-start.7 = (bf16[1,128,512]{2,1,0:T(8,128)(2,1)S(1)}, bf16[1,128,512]{2,1,0:T(8,128)(2,1)}, u32[]{:S(2)}) copy-start(bf16[1,128,512]{2,1,0:T(8,128)(2,1)} %param.23) | copy-start | bytes 393220
  87.1 8.3 %collective-permute-start.9 = (bf16[128,512]{1,0:T(8,128)(2,1)S(1)}, bf16[128,512]{1,0:T(8,128)(2,1)S(1)}, u32[]{:S(2)}, u32[]{:S(2)}) collective-permute-start(bf16[128,512]{1,0:T(8,128)(2,1)S(1)} %shard_map.140.refs_2_.refs_4_), channel_id=1, source_target_pairs={{0,6},{1,7},{2,4},{3,5},{4,2},{5,3},{6,0},{7,1},{8,14},{9,15},{10,... | collective-permute-start | bytes 393224 | tf_op jit(solution)/shard_map/ppermute | solution.py:407
  87.9 13.2 %collective-permute-start.8 = (bf16[128,512]{1,0:T(8,128)(2,1)S(1)}, bf16[128,512]{1,0:T(8,128)(2,1)S(1)}, u32[]{:S(2)}, u32[]{:S(2)}) collective-permute-start(bf16[128,512]{1,0:T(8,128)(2,1)S(1)} %shard_map.140.refs_2_.refs_4_), channel_id=1, source_target_pairs={{0,4},{1,5},{2,6},{3,7},{4,0},{5,1},{6,2},{7,3},{8,12},{9,13},{10,... | collective-permute-start | bytes 393224 | tf_op jit(solution)/shard_map/ppermute | solution.py:407
  89.1 12.0 %collective-permute-start.7 = (bf16[128,512]{1,0:T(8,128)(2,1)S(1)}, bf16[128,512]{1,0:T(8,128)(2,1)S(1)}, u32[]{:S(2)}, u32[]{:S(2)}) collective-permute-start(bf16[128,512]{1,0:T(8,128)(2,1)S(1)} %shard_map.140.refs_2_.refs_4_), channel_id=1, source_target_pairs={{0,2},{1,3},{2,0},{3,1},{4,6},{5,7},{6,4},{7,5},{8,10},{9,11},{10,... | collective-permute-start | bytes 393224 | tf_op jit(solution)/shard_map/ppermute | solution.py:407
  91.6 10.0 %collective-permute-start.10 = (bf16[128,512]{1,0:T(8,128)(2,1)S(1)}, bf16[128,512]{1,0:T(8,128)(2,1)S(1)}, u32[]{:S(2)}, u32[]{:S(2)}) collective-permute-start(bf16[128,512]{1,0:T(8,128)(2,1)S(1)} %shard_map.140.refs_2_.refs_4_), channel_id=1, source_target_pairs={{0,1},{1,0},{2,3},{3,2},{4,5},{5,4},{6,7},{7,6},{8,9},{9,8},{10,11... | collective-permute-start | bytes 393224 | tf_op jit(solution)/shard_map/ppermute | solution.py:407
  95.5 6.1 %collective-permute-start.13 = (bf16[128,512]{1,0:T(8,128)(2,1)S(1)}, bf16[128,512]{1,0:T(8,128)(2,1)S(1)}, u32[]{:S(2)}, u32[]{:S(2)}) collective-permute-start(bf16[128,512]{1,0:T(8,128)(2,1)S(1)} %collective-permute-done.9.refs_5_.refs_7_), channel_id=1, source_target_pairs={{0,1},{1,0},{2,3},{3,2},{4,5},{5,4},{6,7},{7,6},{8,9},{9,8},{10,11... | collective-permute-start | bytes 393224 | tf_op jit(solution)/shard_map/ppermute | solution.py:407
  101.0 1.3 %collective-permute-start.12 = (bf16[128,512]{1,0:T(8,128)(2,1)S(1)}, bf16[128,512]{1,0:T(8,128)(2,1)S(1)}, u32[]{:S(2)}, u32[]{:S(2)}) collective-permute-start(bf16[128,512]{1,0:T(8,128)(2,1)S(1)} %collective-permute-done.8.refs_4_.refs_6_), channel_id=1, source_target_pairs={{0,1},{1,0},{2,3},{3,2},{4,5},{5,4},{6,7},{7,6},{8,9},{9,8},{10,11... | collective-permute-start | bytes 393224 | tf_op jit(solution)/shard_map/ppermute | solution.py:407
  101.1 1.5 %collective-permute-start.11 = (bf16[128,512]{1,0:T(8,128)(2,1)S(1)}, bf16[128,512]{1,0:T(8,128)(2,1)S(1)}, u32[]{:S(2)}, u32[]{:S(2)}) collective-permute-start(bf16[128,512]{1,0:T(8,128)(2,1)S(1)} %collective-permute-done.7.refs_3_.refs_5_), channel_id=1, source_target_pairs={{0,1},{1,0},{2,3},{3,2},{4,5},{5,4},{6,7},{7,6},{8,9},{9,8},{10,11... | collective-permute-start | bytes 393224 | tf_op jit(solution)/shard_map/ppermute | solution.py:407
  105.0 9.2 %collective-permute-start.14 = (bf16[256,512]{1,0:T(8,128)(2,1)S(1)}, bf16[256,512]{1,0:T(8,128)(2,1)S(1)}, u32[]{:S(2)}, u32[]{:S(2)}) collective-permute-start(bf16[256,512]{1,0:T(8,128)(2,1)S(1)} %get-tuple-element.71), channel_id=1, source_target_pairs={{0,8},{8,0},{16,24},{24,16},{1,9},{9,1},{17,25},{25,17},{2,10},{10... | collective-permute-start | bytes 786440 | tf_op jit(solution)/shard_map/ppermute | solution.py:407
  105.6 13.9 %collective-permute-start.15 = (bf16[256,512]{1,0:T(8,128)(2,1)S(1)}, bf16[256,512]{1,0:T(8,128)(2,1)S(1)}, u32[]{:S(2)}, u32[]{:S(2)}) collective-permute-start(bf16[256,512]{1,0:T(8,128)(2,1)S(1)} %get-tuple-element.72), channel_id=1, source_target_pairs={{0,16},{8,24},{16,0},{24,8},{1,17},{9,25},{17,1},{25,9},{2,18},{10... | collective-permute-start | bytes 786440 | tf_op jit(solution)/shard_map/ppermute | solution.py:407
  107.9 11.7 %collective-permute-start.16 = (bf16[256,512]{1,0:T(8,128)(2,1)S(1)}, bf16[256,512]{1,0:T(8,128)(2,1)S(1)}, u32[]{:S(2)}, u32[]{:S(2)}) collective-permute-start(bf16[256,512]{1,0:T(8,128)(2,1)S(1)} %shard_map.143), channel_id=1, source_target_pairs={{0,24},{8,16},{16,8},{24,0},{1,25},{9,17},{17,9},{25,1},{2,26},{10... | collective-permute-start | bytes 786440 | tf_op jit(solution)/shard_map/ppermute | solution.py:407
where the time goes:
time: 121 us
  blocking collectives  38.4 us (32%)
  waiting for transfers between devices  35.1 us (29%)
  Pallas kernels  25.3 us (21%)
  starting transfers between devices  17.7 us (15%)
  local copies, waits for them, and re-layouts  3.18 us (3%)
    all_to_all x4, blocking collectives, exchange(): return lax.all_to_all(value, both, split_axis=0, concat_axis=0, tiled=True)  38.4 us
    ppermute x17, waiting for transfers between devices, swap(): return lax.ppermute(value, axis, [(i, i ^ apart) for i in range(size)])  35.1 us
    pallas_call x14, Pallas kernels, call(): pl.pallas_call(kernel, out_shape=list(outs), in_specs=specs, out_specs=[p...  25.3 us
    ppermute x17, starting transfers between devices, swap(): return lax.ppermute(value, axis, [(i, i ^ apart) for i in range(size)])  17.7 us
    unnamed x20, local copies, waits for them, and re-layouts  3.13 us
  transfers between devices with their start and end apart: 17, of which 12 were waited for; matrix products, arithmetic and copies ran while one was open for 0% of the time, Pallas kernels for 7%

commit v1 on v0

--- a/solution.py
+++ b/solution.py
@@ -12,6 +12,7 @@
 BF16 = jnp.bfloat16
 LANES = 128
 META_ROWS = 16
+CHUNKS = 2
 MIB = 1024 * 1024
 
 
@@ -71,16 +72,23 @@
     )
 
 
-def pack_kernel(block, feat, lens, owner, dst, out, held, own_held, dst_held, sems):
+def pack_kernel(block, feat, weight, lens, owner, dst, *refs):
+    *outs, feat_held, weight_held, held, own_held, dst_held, sems = refs
     rows = feat.shape[0]
-    pairs = ((lens, held), (owner, own_held), (dst, dst_held), (feat, out.at[:rows, :]))
+    pairs = (
+        (feat, feat_held),
+        (weight, weight_held),
+        (lens, held),
+        (owner, own_held),
+        (dst, dst_held),
+    )
     copies = [
         pltpu.make_async_copy(source, target, sems.at[i])
         for i, (source, target) in enumerate(pairs)
     ]
     for copy in copies:
         copy.start()
-    for copy in copies[:3]:
+    for copy in copies[2:]:
         copy.wait()
     high, middle = halves(held[...])
     low = (held[...] - high.astype(F32) - middle.astype(F32)).astype(BF16)
@@ -90,11 +98,13 @@
     found += [v.astype(F32) for v in (own_held[...], section, far - section * block)]
     fill = META_ROWS - 6 * lens.shape[0]
     found.append(jnp.zeros((fill, rows), F32))
-    meta = jnp.concatenate(found, axis=0).astype(BF16)
-    out[rows:, :] = jnp.concatenate(
-        [meta, jnp.zeros((META_ROWS, feat.shape[1] - rows), BF16)], axis=1
-    )
-    copies[3].wait()
+    outs[0][rows:, :] = jnp.concatenate(found, axis=0).astype(BF16)
+    copies[0].wait()
+    copies[1].wait()
+    size = outs[0].shape[1]
+    for c, out in enumerate(outs):
+        pre = dot(feat_held[...], weight_held[:, c * size : (c + 1) * size])
+        out[:rows, :] = pre.astype(BF16)
 
 
 def index_kernel(block, parts, sends, src_row, pick, pick_t, source, source_t):
@@ -125,8 +135,8 @@
         source_t[:, rows] = mark(ids_t == src_row[k : k + 1, :])
 
 
-def edge_data(feat, rows):
-    return feat[rows:, :rows].astype(F32)
+def edge_data(feat, at, rows):
+    return feat[at + rows : at + rows + META_ROWS, :].astype(F32)
 
 
 def edge_length(meta, fanout, k):
@@ -141,21 +151,25 @@
     return jnp.where(where == section, order * block + place, -1)
 
 
-def encode_kernel(count, nodes, block, fanout, rows, last, who, *refs):
-    feats = refs[:count]
-    weight, vec = refs[count : count + 2]
+def encode_kernel(spans, nodes, block, fanout, rows, chunk, last, who, *refs):
+    count = len(spans)
+    feats, metas = refs[:count], refs[count : 2 * count]
+    vec = refs[2 * count]
     if last:
-        before, keep, cross, message, spots = refs[count + 2 :]
+        before, keep, cross, message, spots = refs[2 * count + 1 :]
     else:
-        total, message, spots = refs[count + 2 :]
+        total, message, spots = refs[2 * count + 1 :]
     section, node = who[0], who[1]
+    size = feats[0].shape[1]
+    part = vec[:, chunk * size : (chunk + 1) * size]
     for j in range(count):
-        pre = dot(feats[j][:rows, :], weight[...])
-        meta = edge_data(feats[j], rows)
+        at_feat, at_meta = spans[j]
+        pre = feats[j][at_feat : at_feat + rows, :].astype(F32)
+        meta = edge_data(metas[j], at_meta, rows)
         turned = meta.T
         for k in range(fanout):
             at = (j * fanout + k) * rows
-            act = pre + edge_length(turned, fanout, k) * vec[...]
+            act = pre + edge_length(turned, fanout, k) * part
             message[at : at + rows, :] = silu(act).astype(BF16)
             spots[:, at : at + rows] = spot_of(
                 lambda t, meta=meta: meta[t : t + 1], fanout, k, section, node, nodes, block
@@ -164,28 +178,31 @@
     step = min(half, 512)
     for out, base in ((cross, half), (keep, 0)) if last else ((total, 0),):
 
-        def chunk(c, carry, out=out, base=base):
+        def piece(c, carry, out=out, base=base):
             start = pl.multiple_of(c * step, step)
             ids = iota((step, spots.shape[1]), 0) + (base + start)
-            part = dot(mark(ids == spots[...]), message[...])
+            found = dot(mark(ids == spots[...]), message[...])
             if last:
-                part = part + before[pl.ds(base + start, step), :]
-            out[pl.ds(start, step), :] = part.astype(out.dtype)
+                found = found + before[pl.ds(base + start, step), :]
+            out[pl.ds(start, step), :] = found.astype(out.dtype)
             return carry
 
-        lax.fori_loop(0, out.shape[0] // step, chunk, 0)
-
-
-def slope_kernel(sects, fanout, rows, *refs):
-    feats = refs[:sects]
-    weight, vec = refs[sects : sects + 2]
-    outs = refs[sects + 2 :]
-    for j in range(sects):
-        pre = dot(feats[j][:rows, :], weight[...])
-        turned = edge_data(feats[j], rows).T
+        lax.fori_loop(0, out.shape[0] // step, piece, 0)
+
+
+def slope_kernel(spans, chunks, fanout, rows, *refs):
+    count = len(spans)
+    feats, vec, outs = refs[:count], refs[count], refs[count + 1 :]
+    size = feats[0].shape[1]
+    for i, at in enumerate(spans):
+        c = i % chunks
+        if c == 0:
+            turned = edge_data(feats[i], at, rows).T
+        pre = feats[i][at : at + rows, :].astype(F32)
+        part = vec[:, c * size : (c + 1) * size]
         for k in range(fanout):
-            act = pre + edge_length(turned, fanout, k) * vec[...]
-            outs[j][k * rows : (k + 1) * rows, :] = slope(act).astype(BF16)
+            act = pre + edge_length(turned, fanout, k) * part
+            outs[i][k * rows : (k + 1) * rows, :] = slope(act).astype(BF16)
 
 
 def halo_rows(state, pick, parts):
@@ -223,12 +240,16 @@
     return jnp.concatenate([total[i * block : (i + 1) * block] for i in range(parts)], axis=1)
 
 
-def start_kernel(parts, sums, *refs):
-    received, (init, weight, pick, state, mesh_pre, halo) = refs[:-6], refs[-6:]
-    agg = sums[...]
-    for ref in received:
-        agg = agg + ref[...].astype(F32)
-    pre = dot(agg.astype(BF16), weight[...])
+def start_kernel(parts, chunks, *refs):
+    sums, (init, weight, pick, state, mesh_pre, halo) = refs[:-6], refs[-6:]
+    count = len(sums) // chunks
+    found = []
+    for c in range(chunks):
+        agg = sums[c * count][...]
+        for ref in sums[c * count + 1 : (c + 1) * count]:
+            agg = agg + ref[...].astype(F32)
+        found.append(agg.astype(BF16))
+    pre = dot(jnp.concatenate(found, axis=1), weight[...])
     mesh_pre[...] = pre
     new = (init[...].astype(F32) + silu(pre)).astype(BF16)
     state[...] = new
@@ -333,20 +354,24 @@
     grad_halo[...] = cut_pieces(sent.astype(BF16), parts)
 
 
-def mesh_back_kernel(parts, mine, returned, pick_t, mesh_pre, weight, out):
+def mesh_back_kernel(parts, mine, returned, pick_t, mesh_pre, weight, *outs):
     block = mine.shape[0]
     grad = mine[...] + add_pieces(returned[...], pick_t[...], block, parts)
-    out[...] = back_dot(grad * slope(mesh_pre[...]), weight[...]).astype(BF16)
-
-
-def message_back_kernel(nodes, block, fanout, count, who, *refs):
-    feats, slopes = refs[:count], refs[count : 2 * count]
-    grads, outs = refs[2 * count : -count], refs[-count:]
-    rows = outs[0].shape[0]
+    found = back_dot(grad * slope(mesh_pre[...]), weight[...]).astype(BF16)
+    size = outs[0].shape[1]
+    for c, out in enumerate(outs):
+        out[...] = found[:, c * size : (c + 1) * size]
+
+
+def message_back_kernel(nodes, block, fanout, spans, who, *refs):
+    count = len(spans)
+    metas, slopes = refs[:count], refs[count : 2 * count]
+    same, other, out = refs[2 * count :]
+    rows = out.shape[0] // count
     ids = iota((rows, nodes * block), 1)
     marks = []
-    for feat in feats:
-        turned = edge_data(feat, rows).T
+    for meta, at in zip(metas, spans):
+        turned = edge_data(meta, at, rows).T
         for k in range(fanout):
             spot = spot_of(
                 lambda t, turned=turned: turned[:, t : t + 1],
@@ -359,23 +384,27 @@
             )
             marks.append(mark(ids == spot))
     picked = dot(
-        jnp.concatenate(marks, axis=0), jnp.concatenate([ref[...] for ref in grads], axis=0)
-    )
-    for j, out in enumerate(outs):
-        total = jnp.zeros(out.shape, F32)
+        jnp.concatenate(marks, axis=0), jnp.concatenate([same[...], other[...]], axis=0)
+    )
+    for j in range(count):
+        total = jnp.zeros((rows, out.shape[1]), F32)
         for k in range(fanout):
             at = (j * fanout + k) * rows
             part = slopes[j][k * rows : (k + 1) * rows, :].astype(F32)
             total = total + picked[at : at + rows] * part
-        out[...] = total.astype(out.dtype)
-
-
-def grid_back_kernel(*refs):
+        out[j * rows : (j + 1) * rows, :] = total.astype(out.dtype)
+
+
+def grid_back_kernel(chunks, *refs):
     *parts, weight, out = refs
-    total = parts[0][...].astype(F32)
-    for ref in parts[1:]:
-        total = total + ref[...].astype(F32)
-    out[...] = back_dot(total, weight[...]).astype(BF16)
+    count = len(parts) // chunks
+    found = []
+    for c in range(chunks):
+        total = parts[c * count][...].astype(F32)
+        for ref in parts[c * count + 1 : (c + 1) * count]:
+            total = total + ref[...].astype(F32)
+        found.append(total)
+    out[...] = back_dot(jnp.concatenate(found, axis=1), weight[...]).astype(BF16)
 
 
 def call(kernel, outs, args, smem=0, scratch=(), macs=0, scalars=0, space=pltpu.VMEM):
@@ -392,7 +421,7 @@
         scratch_shapes=list(scratch),
         compiler_params=pltpu.CompilerParams(vmem_limit_bytes=limit),
         cost_estimate=pl.CostEstimate(
-            flops=2 * macs, bytes_accessed=moved, transcendentals=scalars
+            flops=1, bytes_accessed=1, transcendentals=0
         ),
     )(*args)
     return result
@@ -405,6 +434,25 @@
 def swap(value, axis, apart):
     size = lax.axis_size(axis)
     return lax.ppermute(value, axis, [(i, i ^ apart) for i in range(size)])
+
+
+def halving(value, axis, unit, count):
+    while count > 1:
+        count //= 2
+        rows = value.shape[0] // 2
+        given = swap(value[rows:].astype(BF16), axis, unit * count)
+        if count == 1:
+            return value[:rows], given
+        value = value[:rows] + given.astype(F32)
+    return (value,)
+
+
+def doubling(value, axis, unit, count):
+    apart = 1
+    while apart < count:
+        value = jnp.concatenate([value, swap(value, axis, unit * apart)], axis=0)
+        apart *= 2
+    return value
 
 
 def body(
@@ -430,41 +478,72 @@
     both = ("sect", "node")
     who = jnp.stack([lax.axis_index("sect"), lax.axis_index("node")]).astype(jnp.int32)
 
+    chunks = CHUNKS
+    size = width // chunks
     ends = pltpu.VMEM((fanout, grid_rows), jnp.int32)
-    (packed,) = call(
+    packed = call(
         functools.partial(pack_kernel, block),
-        [shape((grid_rows + META_ROWS, width), BF16)],
+        [
+            shape((grid_rows + (0 if c else META_ROWS), size), BF16)
+            for c in range(chunks)
+        ],
         [
             pltpu.with_memory_space_constraint(value, pltpu.HBM)
-            for value in (grid_feat, edge_len.T, g2m_owner.T, g2m_dst.T)
+            for value in (grid_feat, enc_weight, edge_len.T, g2m_owner.T, g2m_dst.T)
         ],
         scratch=[
+            pltpu.VMEM((grid_rows, width), BF16),
+            pltpu.VMEM((width, width), BF16),
             pltpu.VMEM((fanout, grid_rows), F32),
             ends,
             ends,
-            pltpu.SemaphoreType.DMA((4,)),
+            pltpu.SemaphoreType.DMA((5,)),
         ],
+        macs=grid_rows * width * width,
         space=pltpu.HBM,
     )
-    feats = [packed] + [swap(packed, "sect", j) for j in range(1, sects)]
+    axes = [1 << i for i in range(sects.bit_length() - 1)]
+    feats = []
+    for c, part in enumerate(packed):
+        rows = part.shape[0]
+        found, names, held = {0: (part, 0)}, [0], part
+        for axis in axes[::-1] if c % 2 else axes:
+            if len(names) > 1:
+                held = jnp.concatenate([held, given], axis=0)
+            given = swap(held, "sect", axis)
+            for i, j in enumerate(list(names)):
+                found[j ^ axis] = (given, i * rows)
+                names.append(j ^ axis)
+        feats.append(found)
+    metas = feats[0]
     vec = enc_vec[None, :]
     half = nodes // 2
 
-    def encode(used, last, outs, extra):
-        edges = len(used) * grid_rows * fanout
+    def encode(js, c, last, outs, extra):
+        edges = len(js) * grid_rows * fanout
+        spans = tuple((feats[c][j][1], metas[j][1]) for j in js)
         return call(
             functools.partial(
-                encode_kernel, len(used), nodes, block, fanout, grid_rows, last
+                encode_kernel, spans, nodes, block, fanout, grid_rows, c, last
             ),
             outs,
-            [who, *used, enc_weight, vec, *extra],
+            [
+                who,
+                *(feats[c][j][0] for j in js),
+                *(metas[j][0] for j in js),
+                vec,
+                *extra,
+            ],
             smem=1,
-            scratch=[pltpu.VMEM((edges, width), BF16), pltpu.VMEM((1, edges), jnp.int32)],
-            macs=len(used) * grid_rows * width * width + edges * nodes * block * width,
-            scalars=edges * width,
+            scratch=[pltpu.VMEM((edges, size), BF16), pltpu.VMEM((1, edges), jnp.int32)],
+            macs=edges * nodes * block * size,
+            scalars=edges * size,
         )
 
-    before = encode(feats[:1], False, [shape((nodes * block, width), F32)], [])
+    before = [
+        encode([0], c, False, [shape((nodes * block, size), F32)], [])[0]
+        for c in range(chunks)
+    ]
     sends = halo_send[0, 0].transpose(0, 2, 1)
     src_row = mesh_src[0].T
     fan = src_row.shape[0]
@@ -482,23 +561,30 @@
         scalars=4 * fan * block * table_len,
     )
     *before, pick, pick_t, source, source_t = lax.optimization_barrier((*before, *found))
-    keep, cross = encode(
-        feats[1:], True, [shape((half * block, width), BF16)] * 2, before
-    )
-
-    pair = keep.astype(F32) + swap(cross, "node", 1).astype(F32)
-    pair = pair.reshape(half, block, width)
-    arrived = [swap(pair[q].astype(BF16), "node", 2 * q) for q in range(1, half)]
-
+
+    sums = []
+    for c in range(chunks):
+        keep, cross = encode(
+            list(range(1, sects)),
+            c,
+            True,
+            [shape((half * block, size), BF16)] * 2,
+            [before[c]],
+        )
+        pair = keep.astype(F32) + swap(cross, "node", 1).astype(F32)
+        sums.append(halving(pair, "node", 2, half))
+    sums = [value for pieces_of in sums for value in pieces_of]
+    every = [feats[c][j] for j in range(sects) for c in range(chunks)]
     slopes = call(
-        functools.partial(slope_kernel, sects, fanout, grid_rows),
-        [shape((fanout * grid_rows, width), BF16)] * sects,
-        [*feats, enc_weight, vec],
-        macs=sects * grid_rows * width * width,
+        functools.partial(
+            slope_kernel, tuple(at for _, at in every), chunks, fanout, grid_rows
+        ),
+        [shape((fanout * grid_rows, size), BF16)] * (sects * chunks),
+        [*(part for part, _ in every), vec],
         scalars=sects * grid_rows * fanout * width,
     )
-    tied = lax.optimization_barrier((*arrived, *slopes))
-    arrived, slopes = tied[: half - 1], tied[half - 1 :]
+    tied = lax.optimization_barrier((*sums, *slopes))
+    sums, slopes = tied[: len(sums)], tied[len(sums) :]
 
     halo_shape = shape((pieces, LANES), BF16)
     row_low, row_high = shape((block, width), BF16), shape((block, width), F32)
@@ -507,9 +593,9 @@
         return lax.all_to_all(value, both, split_axis=0, concat_axis=0, tiled=True)
 
     state, mesh_pre, halo = call(
-        functools.partial(start_kernel, parts),
+        functools.partial(start_kernel, parts, chunks),
         [row_low, row_high, halo_shape],
-        [pair[0], *arrived, mesh_init[0], mesh_weight, pick],
+        [*sums, mesh_init[0], mesh_weight, pick],
         macs=block * width * width,
         scalars=block * width,
     )
@@ -536,32 +622,53 @@
         macs=2 * layer_macs,
         scalars=block * width,
     )
-    (grad_sum,) = call(
+    grad_sums = call(
         functools.partial(mesh_back_kernel, parts),
-        [row_low],
+        [shape((block, size), BF16)] * chunks,
         [grad, exchange(halo), pick_t, mesh_pre, mesh_weight],
         macs=2 * block * width * width,
         scalars=block * width,
     )
 
-    same = [grad_sum] + [swap(grad_sum, "node", 2 * q) for q in range(1, half)]
-    other = [swap(rows, "node", 1) for rows in same]
-    parts_of = {}
-    for group in ([sects - 1], list(range(1, sects - 1)), [0]):
-        found = call(
-            functools.partial(message_back_kernel, nodes, block, fanout, len(group)),
-            [shape((grid_rows, width), BF16)] * len(group),
-            [who, *(feats[j] for j in group), *(slopes[j] for j in group), *same, *other],
-            smem=1,
-            macs=len(group) * fanout * grid_rows * nodes * block * width,
-        )
-        for j, grad_pre in zip(group, found):
-            parts_of[j] = swap(grad_pre, "sect", j) if j else grad_pre
-    mine, *sent = (parts_of[j] for j in range(sects))
+    total = []
+    ahead = []
+    for c, part in enumerate(grad_sums):
+        same = doubling(part, "node", 2, half)
+        other = swap(same, "node", 1)
+        order = axes[::-1] if c % 2 else axes
+        held = {}
+        for sent in (True, False):
+            group = [j for j in range(sects) if bool(j & order[0]) == sent]
+            same, *_ = lax.optimization_barrier((same, *ahead))
+            spans = tuple(metas[j][1] for j in group)
+            found = call(
+                functools.partial(message_back_kernel, nodes, block, fanout, spans),
+                [shape((len(group) * grid_rows, size), BF16)],
+                [
+                    who,
+                    *(metas[j][0] for j in group),
+                    *(slopes[j * chunks + c] for j in group),
+                    same,
+                    other,
+                ],
+                smem=1,
+                macs=len(group) * fanout * grid_rows * nodes * block * size,
+            )
+            held[sent] = found[0]
+            ahead = [found[0], *total[:1]] if sent else [found[0]]
+        value, given = held[False], swap(held[True], "sect", order[0])
+        for axis in order[1:]:
+            left = [j for j in range(sects) if not any(j & a for a in order[: order.index(axis)])]
+            value = value.astype(F32) + given.astype(F32)
+            rows = {j: value[i * grid_rows : (i + 1) * grid_rows] for i, j in enumerate(left)}
+            sent = jnp.concatenate([rows[j] for j in left if j & axis], axis=0).astype(BF16)
+            value = jnp.concatenate([rows[j] for j in left if not j & axis], axis=0)
+            given = swap(sent, "sect", axis)
+        total += [value, given]
     (grid_grad,) = call(
-        grid_back_kernel,
+        functools.partial(grid_back_kernel, chunks),
         [shape((grid_rows, width), BF16)],
-        [mine, *sent, enc_weight],
+        [*total, enc_weight],
         macs=2 * grid_rows * width * width,
     )
     return (mesh_out[None], grid_grad)

time: 121 us -> 134 us (1.11)
  waiting for transfers between devices: 35.1 us -> 42.6 us
  Pallas kernels: 25.3 us -> 29.4 us
  local copies, waits for them, and re-layouts: 3.18 us -> 1.59 us
  starting transfers between devices: 17.7 us -> 19.2 us
    ppermute x17 -> x20, waiting for transfers between devices: 35.1 us -> 42.6 us  [swap(): return lax.ppermute(value, axis, [(i, i ^ apart) for i in range(size)])]
    pallas_call x14 -> x17, Pallas kernels: 25.3 us -> 29.4 us  [call(): pl.pallas_call(kernel, out_shape=list(outs), in_specs=specs, out_specs=[p...]
    unnamed x20 -> x23, local copies, waits for them, and re-layouts: 3.13 us -> 1.43 us
    ppermute x17 -> x20, starting transfers between devices: 17.7 us -> 19.2 us  [swap(): return lax.ppermute(value, axis, [(i, i ^ apart) for i in range(size)])]
  transfers between devices with their start and end apart: 17 -> 20, of which waited for: 12 -> 12; matrix products, arithmetic and copies ran while one was open for 0% -> 0% of each run, Pallas kernels for 7% -> 13%
where the time goes in v1:
time: 134 us
  waiting for transfers between devices  42.6 us (32%)
  blocking collectives  39.3 us (29%)
  Pallas kernels  29.4 us (22%)
  starting transfers between devices  19.2 us (14%)
  local copies, waits for them, and re-layouts  1.59 us (1%)
    ppermute x20, waiting for transfers between devices, swap(): return lax.ppermute(value, axis, [(i, i ^ apart) for i in range(size)])  42.6 us
    all_to_all x4, blocking collectives, exchange(): return lax.all_to_all(value, both, split_axis=0, concat_axis=0, tiled=True)  39.3 us
    pallas_call x17, Pallas kernels, call(): pl.pallas_call(kernel, out_shape=list(outs), in_specs=specs, out_specs=[p...  29.4 us
    ppermute x20, starting transfers between devices, swap(): return lax.ppermute(value, axis, [(i, i ^ apart) for i in range(size)])  19.2 us
  transfers between devices with their start and end apart: 20, of which 12 were waited for; matrix products, arithmetic and copies ran while one was open for 0% of the time, Pallas kernels for 13%

profile of v1, /device:TPU:0, one launch (start us, length us, event | category | flops | bytes accessed | tf_op | source)
XLA Modules:
  0.0 133.5 jit_solution(2976297413257553428)
XLA Ops:
  0.6 0.0 copy-start.7
  0.7 1.5 %shard_map.131 = (bf16[272,256]{1,0:T(8,128)(2,1)S(1)}, bf16[256,256]{1,0:T(8,128)(2,1)S(1)}) custom-call(bf16[256,512]{1,0:T(8,128)(2,1)} %feat.1, bf16[512,512]{1,0:T(8,128)(2,1)} %refs_4_.1, f32[2,256]{1,0:T(2,128)} %bitcast.40, s32[2,256]{1,0:T(2,128)} %bitcast.41, s32[2,256]{1,0:T(2,128)} %bitcast.42), custom_call_target="tpu_custom_call" | custom-call | flops 1 | bytes 1 | tf_op jit(solution)/shard_map/pallas_call | solution.py:416
  2.2 3.0 %collective-permute-start = (bf16[272,256]{1,0:T(8,128)(2,1)S(1)}, bf16[272,256]{1,0:T(8,128)(2,1)S(1)}, u32[]{:S(2)}, u32[]{:S(2)}) collective-permute-start(bf16[272,256]{1,0:T(8,128)(2,1)S(1)} %get-tuple-element.55.refs_0_.refs_1_), channel_id=1, source_target_pairs={{0,8},{8,0},{16,24},{24,16},{1,9},{9,1},{17,25},{25,17},{2,10},{10... | collective-permute-start | bytes 417800 | tf_op jit(solution)/shard_map/ppermute | solution.py:436
  5.2 1.5 %collective-permute-start.5 = (bf16[256,256]{1,0:T(8,128)(2,1)S(1)}, bf16[256,256]{1,0:T(8,128)(2,1)S(1)}, u32[]{:S(2)}, u32[]{:S(2)}) collective-permute-start(bf16[256,256]{1,0:T(8,128)(2,1)S(1)} %get-tuple-element.56.refs_0_.refs_1_), channel_id=1, source_target_pairs={{0,16},{8,24},{16,0},{24,8},{1,17},{9,25},{17,1},{25,9},{2,18},{10... | collective-permute-start | bytes 393224 | tf_op jit(solution)/shard_map/ppermute | solution.py:436
  6.7 2.2 %collective-permute-done.refs_0_.refs_3_.refs_2_.refs_1_ = bf16[272,256]{1,0:T(8,128)(2,1)S(1)} collective-permute-done((bf16[272,256]{1,0:T(8,128)(2,1)S(1)}, bf16[272,256]{1,0:T(8,128)(2,1)S(1)}, u32[]{:S(2)}, u32[]{:S(2)}) %collective-permute-start) | collective-permute-done | bytes 139296 | tf_op jit(solution)/shard_map/ppermute | solution.py:436
  8.9 1.8 %collective-permute-start.1 = (bf16[544,256]{1,0:T(8,128)(2,1)S(1)}, bf16[544,256]{1,0:T(8,128)(2,1)S(1)}, u32[]{:S(2)}, u32[]{:S(2)}) collective-permute-start(bf16[544,256]{1,0:T(8,128)(2,1)S(1)} %pad_maximum_fusion), channel_id=1, source_target_pairs={{0,16},{8,24},{16,0},{24,8},{1,17},{9,25},{17,1},{25,9},{2,18},{10... | collective-permute-start | bytes 835592 | tf_op jit(solution)/shard_map/ppermute | solution.py:436
  10.7 1.6 %collective-permute-start.6 = (bf16[512,256]{1,0:T(8,128)(2,1)S(1)}, bf16[512,256]{1,0:T(8,128)(2,1)S(1)}, u32[]{:S(2)}, u32[]{:S(2)}) collective-permute-start(bf16[512,256]{1,0:T(8,128)(2,1)S(1)} %pad_maximum_fusion.1), channel_id=1, source_target_pairs={{0,8},{8,0},{16,24},{24,16},{1,9},{9,1},{17,25},{25,17},{2,10},{10... | collective-permute-start | bytes 786440 | tf_op jit(solution)/shard_map/ppermute | solution.py:436
  12.3 0.1 pad_add_fusion.who
  12.3 0.7 copy-done.5
  13.0 1.5 %shard_map.133.refs_7_ = f32[1024,256]{1,0:T(8,128)S(1)} custom-call(s32[2]{0:T(128)S(1)} %pad_add_fusion.who, bf16[256,256]{1,0:T(8,128)(2,1)S(1)} %get-tuple-element.56.refs_0_.refs_1_, bf16[272,256]{1,0:T(8,128)(2,1)S(1)} %get-tuple-element.55.refs_0_.refs_1_, f32[1,512]{1,0:T(1,128)S(1)} %bitcast.33), custom_call_target="tpu_custom_call" | custom-call | flops 1 | bytes 1 | tf_op jit(solution)/shard_map/pallas_call | solution.py:416
  14.5 0.0 copy-start.6
  14.5 0.7 copy-done.6
  15.2 1.5 %shard_map.132.refs_7_ = f32[1024,256]{1,0:T(8,128)S(1)} custom-call(s32[2]{0:T(128)S(1)} %pad_add_fusion.who, bf16[272,256]{1,0:T(8,128)(2,1)S(1)} %get-tuple-element.55.refs_0_.refs_1_, bf16[272,256]{1,0:T(8,128)(2,1)S(1)} %get-tuple-element.55.refs_0_.refs_1_, f32[1,512]{1,0:T(1,128)S(1)} %bitcast.34), custom_call_target="tpu_custom_call" | custom-call | flops 1 | bytes 1 | tf_op jit(solution)/shard_map/pallas_call | solution.py:416
  16.7 0.7 shard_map.134
  17.4 2.1 %shard_map.135 = (bf16[512,256]{1,0:T(8,128)(2,1)S(1)}, bf16[512,256]{1,0:T(8,128)(2,1)S(1)}) custom-call(s32[2]{0:T(128)S(1)} %pad_add_fusion.who, bf16[272,256]{1,0:T(8,128)(2,1)S(1)} %collective-permute-done.refs_0_.refs_3_.refs_2_.refs_1_, bf16[544,256]{1,0:T(8,128)(2,1)S(1)} %collective-permute-done.1.refs_1_.refs_2_.refs_4_.refs_5_.refs_6_.refs_0_, ...), custom_call_target="tpu_custom_call" | custom-call | flops 1 | bytes 1 | tf_op jit(solution)/shard_map/pallas_call | solution.py:416
  19.6 0.0 copy-start.2
  19.6 0.1 collective-permute-start.2
  19.7 2.1 %shard_map.136 = (bf16[512,256]{1,0:T(8,128)(2,1)S(1)}, bf16[512,256]{1,0:T(8,128)(2,1)S(1)}) custom-call(s32[2]{0:T(128)S(1)} %pad_add_fusion.who, bf16[512,256]{1,0:T(8,128)(2,1)S(1)} %collective-permute-done.6.refs_0_.refs_2_.refs_3_.refs_7_, bf16[256,256]{1,0:T(8,128)(2,1)S(1)} %collective-permute-done.5.refs_1_.refs_5_, ...), custom_call_target="tpu_custom_call" | custom-call | flops 1 | bytes 1 | tf_op jit(solution)/shard_map/pallas_call | solution.py:416
  21.8 0.6 collective-permute-start.7
  22.4 0.1 convert_add_fusion.3
  22.4 2.7 %collective-permute-start.3 = (bf16[256,256]{1,0:T(8,128)(2,1)S(1)}, bf16[256,256]{1,0:T(8,128)(2,1)S(1)}, u32[]{:S(2)}, u32[]{:S(2)}) collective-permute-start(bf16[256,256]{1,0:T(8,128)(2,1)S(1)} %slice.77), channel_id=1, source_target_pairs={{0,4},{1,5},{2,6},{3,7},{4,0},{5,1},{6,2},{7,3},{8,12},{9,13},{10,... | collective-permute-start | bytes 393224 | tf_op jit(solution)/shard_map/ppermute | solution.py:436
  25.1 0.1 convert_add_fusion.2
  25.2 1.1 collective-permute-start.8
  26.3 9.1 %collective-permute-done.3 = bf16[256,256]{1,0:T(8,128)(2,1)S(1)} collective-permute-done((bf16[256,256]{1,0:T(8,128)(2,1)S(1)}, bf16[256,256]{1,0:T(8,128)(2,1)S(1)}, u32[]{:S(2)}, u32[]{:S(2)}) %collective-permute-start.3) | collective-permute-done | bytes 131104 | tf_op jit(solution)/shard_map/ppermute | solution.py:436
  35.4 0.1 collective-permute-start.4
  35.5 1.9 %collective-permute-done.8 = bf16[256,256]{1,0:T(8,128)(2,1)S(1)} collective-permute-done((bf16[256,256]{1,0:T(8,128)(2,1)S(1)}, bf16[256,256]{1,0:T(8,128)(2,1)S(1)}, u32[]{:S(2)}, u32[]{:S(2)}) %collective-permute-start.8) | collective-permute-done | bytes 131104 | tf_op jit(solution)/shard_map/ppermute | solution.py:436
  37.4 0.6 collective-permute-start.9
  38.1 2.0 %shard_map.137 = (bf16[512,256]{1,0:T(8,128)(2,1)S(1)}, bf16[512,256]{1,0:T(8,128)(2,1)S(1)}, bf16[512,256]{1,0:T(8,128)(2,1)S(1)}, bf16[512,256]{1,0:T(8,128)(2...) custom-call(bf16[272,256]{1,0:T(8,128)(2,1)S(1)} %get-tuple-element., ...), custom_call_target="tpu_custom_call" | custom-call | flops 1 | bytes 1 | tf_op jit(solution)/shard_map/pallas_call | solution.py:416
  40.1 0.2 collective-permute-done.4.refs_1_
  40.4 1.4 %collective-permute-done.9.refs_3_ = bf16[128,256]{1,0:T(8,128)(2,1)S(1)} collective-permute-done((bf16[128,256]{1,0:T(8,128)(2,1)S(1)}, bf16[128,256]{1,0:T(8,128)(2,1)S(1)}, u32[]{:S(2)}, u32[]{:S(2)}) %collective-permute-start.9) | collective-permute-done | bytes 65568 | tf_op jit(solution)/shard_map/ppermute | solution.py:436
  41.8 0.5 shard_map.138
  42.2 12.1 %all_to_all.44 = bf16[32,8,128]{2,1,0:T(8,128)(2,1)S(1)} all-to-all(bf16[32,8,128]{2,1,0:T(8,128)(2,1)S(1)} %bitcast.29), channel_id=1, replica_groups=mesh['sect'=4,'node'=8] {'sect','node'}, dimensions={0} | all-to-all | bytes 131072 | tf_op jit(solution)/shard_map/all_to_all | solution.py:593
  54.3 2.2 %shard_map.139 = (bf16[128,512]{1,0:T(8,128)(2,1)S(1)}, f32[128,512]{1,0:T(8,128)S(1)}, bf16[1024,512]{1,0:T(8,128)(2,1)S(1)}, bf16[256,128]{1,0:T(8,128)(2,1)S(1)}) custom-call(bf16[128,512]{1,0:T(8,128)(2,1)S(1)} %get-tuple-element.80.state, bf16[256,128]{1,0:T(8,128)(2,1)S(1)} %bitcast.24, bf16[1024,384]{1,0:T(8,128)(2,1)S(1)} %get-tuple-element.82.source, ...), custom_call_target="tpu_custom_call" | custom-call | flops 1 | bytes 1 | tf_op jit(solution)/shard_map/pallas_call | solution.py:416
  56.5 9.1 %all_to_all.45 = bf16[32,8,128]{2,1,0:T(8,128)(2,1)S(1)} all-to-all(bf16[32,8,128]{2,1,0:T(8,128)(2,1)S(1)} %bitcast.30), channel_id=1, replica_groups=mesh['sect'=4,'node'=8] {'sect','node'}, dimensions={0} | all-to-all | bytes 131072 | tf_op jit(solution)/shard_map/all_to_all | solution.py:593
  65.6 4.3 %shard_map.140 = (bf16[128,512]{1,0:T(8,128)(2,1)}, f32[128,512]{1,0:T(8,128)S(1)}, bf16[256,128]{1,0:T(8,128)(2,1)S(1)}) custom-call(bf16[128,512]{1,0:T(8,128)(2,1)S(1)} %get-tuple-element.83.state, bf16[256,128]{1,0:T(8,128)(2,1)S(1)} %bitcast.25, bf16[1024,384]{1,0:T(8,128)(2,1)S(1)} %get-tuple-element.82.source, ...), custom_call_target="tpu_custom_call" | custom-call | flops 1 | bytes 1 | tf_op jit(solution)/shard_map/pallas_call | solution.py:416
  69.8 9.1 %all_to_all.46 = bf16[32,8,128]{2,1,0:T(8,128)(2,1)S(1)} all-to-all(bf16[32,8,128]{2,1,0:T(8,128)(2,1)S(1)} %bitcast.32), channel_id=1, replica_groups=mesh['sect'=4,'node'=8] {'sect','node'}, dimensions={0} | all-to-all | bytes 131072 | tf_op jit(solution)/shard_map/all_to_all | solution.py:593
  78.9 2.2 %shard_map.141 = (f32[128,512]{1,0:T(8,128)S(1)}, bf16[256,128]{1,0:T(8,128)(2,1)S(1)}) custom-call(f32[128,512]{1,0:T(8,128)S(1)} %get-tuple-element.89.mine, bf16[256,128]{1,0:T(8,128)(2,1)S(1)} %bitcast.23, bf16[512,256]{1,0:T(8,128)(2,1)S(1)} %get-tuple-element.91.pick_t, f32[128,512]{1,0:T(8,128)S(1)} %get-tuple-element.92.mixed, ...), custom_call_target="tpu_custom_call" | custom-call | flops 1 | bytes 1 | tf_op jit(solution)/shard_map/pallas_call | solution.py:416
  81.1 9.1 %all_to_all.47 = bf16[32,8,128]{2,1,0:T(8,128)(2,1)S(1)} all-to-all(bf16[32,8,128]{2,1,0:T(8,128)(2,1)S(1)} %bitcast.31), channel_id=1, replica_groups=mesh['sect'=4,'node'=8] {'sect','node'}, dimensions={0} | all-to-all | bytes 131072 | tf_op jit(solution)/shard_map/all_to_all | solution.py:593
  90.2 0.5 shard_map.142
  90.6 0.5 collective-permute-start.10
  91.1 1.6 %collective-permute-start.15 = (bf16[128,256]{1,0:T(8,128)(2,1)S(1)}, bf16[128,256]{1,0:T(8,128)(2,1)S(1)}, u32[]{:S(2)}, u32[]{:S(2)}) collective-permute-start(bf16[128,256]{1,0:T(8,128)(2,1)S(1)} %get-tuple-element.103), channel_id=1, source_target_pairs={{0,2},{1,3},{2,0},{3,1},{4,6},{5,7},{6,4},{7,5},{8,10},{9,11},{10,... | collective-permute-start | bytes 196616 | tf_op jit(solution)/shard_map/ppermute | solution.py:436
  92.7 2.8 %collective-permute-done.10 = bf16[128,256]{1,0:T(8,128)(2,1)S(1)} collective-permute-done((bf16[128,256]{1,0:T(8,128)(2,1)S(1)}, bf16[128,256]{1,0:T(8,128)(2,1)S(1)}, u32[]{:S(2)}, u32[]{:S(2)}) %collective-permute-start.10) | collective-permute-done | bytes 65568 | tf_op jit(solution)/shard_map/ppermute | solution.py:436
  95.5 0.4 collective-permute-start.11
  96.0 7.0 %collective-permute-done.11 = bf16[256,256]{1,0:T(8,128)(2,1)S(1)} collective-permute-done((bf16[256,256]{1,0:T(8,128)(2,1)S(1)}, bf16[256,256]{1,0:T(8,128)(2,1)S(1)}, u32[]{:S(2)}, u32[]{:S(2)}) %collective-permute-start.11) | collective-permute-done | bytes 131104 | tf_op jit(solution)/shard_map/ppermute | solution.py:436
  103.0 0.1 collective-permute-start.12
  103.1 0.1 collective-permute-start.16
  103.2 7.8 %collective-permute-done.16 = bf16[256,256]{1,0:T(8,128)(2,1)S(1)} collective-permute-done((bf16[256,256]{1,0:T(8,128)(2,1)S(1)}, bf16[256,256]{1,0:T(8,128)(2,1)S(1)}, u32[]{:S(2)}, u32[]{:S(2)}) %collective-permute-start.16) | collective-permute-done | bytes 131104 | tf_op jit(solution)/shard_map/ppermute | solution.py:436
  111.0 0.1 collective-permute-start.17
  111.2 1.8 %shard_map.143 = bf16[512,256]{1,0:T(8,128)(2,1)S(1)} custom-call(s32[2]{0:T(128)S(1)} %pad_add_fusion.who, bf16[272,256]{1,0:T(8,128)(2,1)S(1)} %collective-permute-done.refs_0_.refs_3_.refs_2_.refs_1_, bf16[544,256]{1,0:T(8,128)(2,1)S(1)} %collective-permute-done.1.refs_1_.refs_2_.refs_4_.refs_5_.refs_6_.refs_0_, ...), custom_call_target="tpu_custom_call" | custom-call | flops 1 | bytes 1 | tf_op jit(solution)/shard_map/pallas_call | solution.py:416
  113.0 0.0 copy-start.1
  113.0 0.9 collective-permute-start.13
  113.9 1.8 %shard_map.144 = bf16[512,256]{1,0:T(8,128)(2,1)S(1)} custom-call(s32[2]{0:T(128)S(1)} %pad_add_fusion.who, bf16[272,256]{1,0:T(8,128)(2,1)S(1)} %get-tuple-element.55.refs_0_.refs_1_, bf16[544,256]{1,0:T(8,128)(2,1)S(1)} %collective-permute-done.1.refs_1_.refs_2_.refs_4_.refs_5_.refs_6_.refs_0_, bf16[512,256]{1,0:T(8,128)(2,1)S(1)} %get-tuple-element.87.refs_2_, ...), custom_call_target="tpu_custom_call" | custom-call | flops 1 | bytes 1 | tf_op jit(solution)/shard_map/pallas_call | solution.py:416
  115.8 1.8 %shard_map.145 = bf16[512,256]{1,0:T(8,128)(2,1)S(1)} custom-call(s32[2]{0:T(128)S(1)} %pad_add_fusion.who, bf16[544,256]{1,0:T(8,128)(2,1)S(1)} %collective-permute-done.1.refs_1_.refs_2_.refs_4_.refs_5_.refs_6_.refs_0_, bf16[544,256]{1,0:T(8,128)(2,1)S(1)} %collective-permute-done.1.refs_1_.refs_2_.refs_4_.refs_5_.refs_6_.refs_0_, ...), custom_call_target="tpu_custom_call" | custom-call | flops 1 | bytes 1 | tf_op jit(solution)/shard_map/pallas_call | solution.py:416
  117.6 0.6 collective-permute-start.18
  118.2 3.5 %collective-permute-done.13 = bf16[512,256]{1,0:T(8,128)(2,1)S(1)} collective-permute-done((bf16[512,256]{1,0:T(8,128)(2,1)S(1)}, bf16[512,256]{1,0:T(8,128)(2,1)S(1)}, u32[]{:S(2)}, u32[]{:S(2)}) %collective-permute-start.13) | collective-permute-done | bytes 262176 | tf_op jit(solution)/shard_map/ppermute | solution.py:436
  121.7 0.1 convert_add_fusion.1
  121.8 1.8 %shard_map.146 = bf16[512,256]{1,0:T(8,128)(2,1)S(1)} custom-call(s32[2]{0:T(128)S(1)} %pad_add_fusion.who, bf16[272,256]{1,0:T(8,128)(2,1)S(1)} %get-tuple-element.55.refs_0_.refs_1_, bf16[272,256]{1,0:T(8,128)(2,1)S(1)} %collective-permute-done.refs_0_.refs_3_.refs_2_.refs_1_, bf16[512,256]{1,0:T(8,128)(2,1)S(1)} %get-tuple-element.101.refs_2_, ...), custom_call_target="tpu_custom_call" | custom-call | flops 1 | bytes 1 | tf_op jit(solution)/shard_map/pallas_call | solution.py:416
  123.7 2.4 %collective-permute-done.18 = bf16[512,256]{1,0:T(8,128)(2,1)S(1)} collective-permute-done((bf16[512,256]{1,0:T(8,128)(2,1)S(1)}, bf16[512,256]{1,0:T(8,128)(2,1)S(1)}, u32[]{:S(2)}, u32[]{:S(2)}) %collective-permute-start.18) | collective-permute-done | bytes 262176 | tf_op jit(solution)/shard_map/ppermute | solution.py:436
  126.1 0.1 convert_add_fusion
  126.1 1.2 collective-permute-start.19
  127.4 0.7 collective-permute-start.14
  128.1 3.1 %collective-permute-done.19.refs_3_ = bf16[256,256]{1,0:T(8,128)(2,1)S(1)} collective-permute-done((bf16[256,256]{1,0:T(8,128)(2,1)S(1)}, bf16[256,256]{1,0:T(8,128)(2,1)S(1)}, u32[]{:S(2)}, u32[]{:S(2)}) %collective-permute-start.19) | collective-permute-done | bytes 131104 | tf_op jit(solution)/shard_map/ppermute | solution.py:436
  131.2 1.2 collective-permute-done.14.refs_1_
  132.4 1.2 shard_map.147
  (43 shorter events, 0.3 us)
Async XLA Ops:
  0.6 16.8 %copy-start.7 = (f32[512]{0:T(512)S(1)}, f32[512]{0:T(512)}, u32[]{:S(2)}) copy-start(f32[512]{0:T(512)} %param.17) | copy-start | bytes 6148
  0.6 16.1 %copy-start.9 = (s32[1,128,8]{1,2,0:T(8,128)S(1)}, s32[1,128,8]{1,2,0:T(8,128)}, u32[]{:S(2)}) copy-start(s32[1,128,8]{1,2,0:T(8,128)} %param.21) | copy-start | bytes 12292
  0.7 16.1 %copy-start.8 = (s32[1,1,4,8,2]{3,4,2,1,0:T(2,128)S(1)}, s32[1,1,4,8,2]{3,4,2,1,0:T(2,128)}, u32[]{:S(2)}) copy-start(s32[1,1,4,8,2]{3,4,2,1,0:T(2,128)} %param.20) | copy-start | bytes 772
  2.2 6.7 %collective-permute-start = (bf16[272,256]{1,0:T(8,128)(2,1)S(1)}, bf16[272,256]{1,0:T(8,128)(2,1)S(1)}, u32[]{:S(2)}, u32[]{:S(2)}) collective-permute-start(bf16[272,256]{1,0:T(8,128)(2,1)S(1)} %get-tuple-element.55.refs_0_.refs_1_), channel_id=1, source_target_pairs={{0,8},{8,0},{16,24},{24,16},{1,9},{9,1},{17,25},{25,17},{2,10},{10... | collective-permute-start | bytes 417800 | tf_op jit(solution)/shard_map/ppermute | solution.py:436
  5.2 5.5 %collective-permute-start.5 = (bf16[256,256]{1,0:T(8,128)(2,1)S(1)}, bf16[256,256]{1,0:T(8,128)(2,1)S(1)}, u32[]{:S(2)}, u32[]{:S(2)}) collective-permute-start(bf16[256,256]{1,0:T(8,128)(2,1)S(1)} %get-tuple-element.56.refs_0_.refs_1_), channel_id=1, source_target_pairs={{0,16},{8,24},{16,0},{24,8},{1,17},{9,25},{17,1},{25,9},{2,18},{10... | collective-permute-start | bytes 393224 | tf_op jit(solution)/shard_map/ppermute | solution.py:436
  8.9 8.6 %collective-permute-start.1 = (bf16[544,256]{1,0:T(8,128)(2,1)S(1)}, bf16[544,256]{1,0:T(8,128)(2,1)S(1)}, u32[]{:S(2)}, u32[]{:S(2)}) collective-permute-start(bf16[544,256]{1,0:T(8,128)(2,1)S(1)} %pad_maximum_fusion), channel_id=1, source_target_pairs={{0,16},{8,24},{16,0},{24,8},{1,17},{9,25},{17,1},{25,9},{2,18},{10... | collective-permute-start | bytes 835592 | tf_op jit(solution)/shard_map/ppermute | solution.py:436
  10.7 9.0 %collective-permute-start.6 = (bf16[512,256]{1,0:T(8,128)(2,1)S(1)}, bf16[512,256]{1,0:T(8,128)(2,1)S(1)}, u32[]{:S(2)}, u32[]{:S(2)}) collective-permute-start(bf16[512,256]{1,0:T(8,128)(2,1)S(1)} %pad_maximum_fusion.1), channel_id=1, source_target_pairs={{0,8},{8,0},{16,24},{24,16},{1,9},{9,1},{17,25},{25,17},{2,10},{10... | collective-permute-start | bytes 786440 | tf_op jit(solution)/shard_map/ppermute | solution.py:436
  12.3 0.7 copy-start.5
  14.5 0.7 copy-start.6
  19.6 22.2 %copy-start.2 = (bf16[512,512]{1,0:T(8,128)(2,1)S(1)}, bf16[512,512]{1,0:T(8,128)(2,1)}, u32[]{:S(2)}) copy-start(bf16[512,512]{1,0:T(8,128)(2,1)} %weight.3) | copy-start | bytes 1572868
  19.6 22.2 %copy-start.3 = (bf16[1,128,512]{2,1,0:T(8,128)(2,1)S(1)}, bf16[1,128,512]{2,1,0:T(8,128)(2,1)}, u32[]{:S(2)}) copy-start(bf16[1,128,512]{2,1,0:T(8,128)(2,1)} %param.18) | copy-start | bytes 393220
  19.6 2.8 %collective-permute-start.2 = (bf16[512,256]{1,0:T(8,128)(2,1)S(1)}, bf16[512,256]{1,0:T(8,128)(2,1)S(1)}, u32[]{:S(2)}, u32[]{:S(2)}) collective-permute-start(bf16[512,256]{1,0:T(8,128)(2,1)S(1)} %get-tuple-element.63), channel_id=1, source_target_pairs={{0,1},{1,0},{2,3},{3,2},{4,5},{5,4},{6,7},{7,6},{8,9},{9,8},{10,11... | collective-permute-start | bytes 786440 | tf_op jit(solution)/shard_map/ppermute | solution.py:436
  21.8 32.5 %copy-start = (bf16[2,4,512,512]{3,2,1,0:T(8,128)(2,1)S(1)}, bf16[2,4,512,512]{3,2,1,0:T(8,128)(2,1)}, u32[]{:S(2)}) copy-start(bf16[2,4,512,512]{3,2,1,0:T(8,128)(2,1)} %weights.5) | copy-start | bytes 12582916
  21.8 3.3 %collective-permute-start.7 = (bf16[512,256]{1,0:T(8,128)(2,1)S(1)}, bf16[512,256]{1,0:T(8,128)(2,1)S(1)}, u32[]{:S(2)}, u32[]{:S(2)}) collective-permute-start(bf16[512,256]{1,0:T(8,128)(2,1)S(1)} %get-tuple-element.66), channel_id=1, source_target_pairs={{0,1},{1,0},{2,3},{3,2},{4,5},{5,4},{6,7},{7,6},{8,9},{9,8},{10,11... | collective-permute-start | bytes 786440 | tf_op jit(solution)/shard_map/ppermute | solution.py:436
  22.4 12.9 %collective-permute-start.3 = (bf16[256,256]{1,0:T(8,128)(2,1)S(1)}, bf16[256,256]{1,0:T(8,128)(2,1)S(1)}, u32[]{:S(2)}, u32[]{:S(2)}) collective-permute-start(bf16[256,256]{1,0:T(8,128)(2,1)S(1)} %slice.77), channel_id=1, source_target_pairs={{0,4},{1,5},{2,6},{3,7},{4,0},{5,1},{6,2},{7,3},{8,12},{9,13},{10,... | collective-permute-start | bytes 393224 | tf_op jit(solution)/shard_map/ppermute | solution.py:436
  25.2 12.2 %collective-permute-start.8 = (bf16[256,256]{1,0:T(8,128)(2,1)S(1)}, bf16[256,256]{1,0:T(8,128)(2,1)S(1)}, u32[]{:S(2)}, u32[]{:S(2)}) collective-permute-start(bf16[256,256]{1,0:T(8,128)(2,1)S(1)} %slice.76), channel_id=1, source_target_pairs={{0,4},{1,5},{2,6},{3,7},{4,0},{5,1},{6,2},{7,3},{8,12},{9,13},{10,... | collective-permute-start | bytes 393224 | tf_op jit(solution)/shard_map/ppermute | solution.py:436
  35.4 4.9 %collective-permute-start.4 = (bf16[128,256]{1,0:T(8,128)(2,1)S(1)}, bf16[128,256]{1,0:T(8,128)(2,1)S(1)}, u32[]{:S(2)}, u32[]{:S(2)}) collective-permute-start(bf16[128,256]{1,0:T(8,128)(2,1)S(1)} %slice.79), channel_id=1, source_target_pairs={{0,2},{1,3},{2,0},{3,1},{4,6},{5,7},{6,4},{7,5},{8,10},{9,11},{10,... | collective-permute-start | bytes 196616 | tf_op jit(solution)/shard_map/ppermute | solution.py:436
  37.4 28.2 %copy-start.4 = (bf16[1,128,512]{2,1,0:T(8,128)(2,1)S(1)}, bf16[1,128,512]{2,1,0:T(8,128)(2,1)}, u32[]{:S(2)}) copy-start(bf16[1,128,512]{2,1,0:T(8,128)(2,1)} %param.23) | copy-start | bytes 393220
  37.4 4.3 %collective-permute-start.9 = (bf16[128,256]{1,0:T(8,128)(2,1)S(1)}, bf16[128,256]{1,0:T(8,128)(2,1)S(1)}, u32[]{:S(2)}, u32[]{:S(2)}) collective-permute-start(bf16[128,256]{1,0:T(8,128)(2,1)S(1)} %slice.78), channel_id=1, source_target_pairs={{0,2},{1,3},{2,0},{3,1},{4,6},{5,7},{6,4},{7,5},{8,10},{9,11},{10,... | collective-permute-start | bytes 196616 | tf_op jit(solution)/shard_map/ppermute | solution.py:436
  90.6 4.9 %collective-permute-start.10 = (bf16[128,256]{1,0:T(8,128)(2,1)S(1)}, bf16[128,256]{1,0:T(8,128)(2,1)S(1)}, u32[]{:S(2)}, u32[]{:S(2)}) collective-permute-start(bf16[128,256]{1,0:T(8,128)(2,1)S(1)} %get-tuple-element.97), channel_id=1, source_target_pairs={{0,2},{1,3},{2,0},{3,1},{4,6},{5,7},{6,4},{7,5},{8,10},{9,11},{10,... | collective-permute-start | bytes 196616 | tf_op jit(solution)/shard_map/ppermute | solution.py:436
  91.1 12.0 %collective-permute-start.15 = (bf16[128,256]{1,0:T(8,128)(2,1)S(1)}, bf16[128,256]{1,0:T(8,128)(2,1)S(1)}, u32[]{:S(2)}, u32[]{:S(2)}) collective-permute-start(bf16[128,256]{1,0:T(8,128)(2,1)S(1)} %get-tuple-element.103), channel_id=1, source_target_pairs={{0,2},{1,3},{2,0},{3,1},{4,6},{5,7},{6,4},{7,5},{8,10},{9,11},{10,... | collective-permute-start | bytes 196616 | tf_op jit(solution)/shard_map/ppermute | solution.py:436
  95.5 7.5 %collective-permute-start.11 = (bf16[256,256]{1,0:T(8,128)(2,1)S(1)}, bf16[256,256]{1,0:T(8,128)(2,1)S(1)}, u32[]{:S(2)}, u32[]{:S(2)}) collective-permute-start(bf16[256,256]{1,0:T(8,128)(2,1)S(1)} %pad_maximum_fusion.2), channel_id=1, source_target_pairs={{0,4},{1,5},{2,6},{3,7},{4,0},{5,1},{6,2},{7,3},{8,12},{9,13},{10,... | collective-permute-start | bytes 393224 | tf_op jit(solution)/shard_map/ppermute | solution.py:436
  103.0 8.2 %collective-permute-start.12 = (bf16[512,256]{1,0:T(8,128)(2,1)S(1)}, bf16[512,256]{1,0:T(8,128)(2,1)S(1)}, u32[]{:S(2)}, u32[]{:S(2)}) collective-permute-start(bf16[512,256]{1,0:T(8,128)(2,1)S(1)} %constant_dynamic-update-slice_fusion.refs_4_), channel_id=1, source_target_pairs={{0,1},{1,0},{2,3},{3,2},{4,5},{5,4},{6,7},{7,6},{8,9},{9,8},{10,11... | collective-permute-start | bytes 786440 | tf_op jit(solution)/shard_map/ppermute | solution.py:436
  103.1 7.9 %collective-permute-start.16 = (bf16[256,256]{1,0:T(8,128)(2,1)S(1)}, bf16[256,256]{1,0:T(8,128)(2,1)S(1)}, u32[]{:S(2)}, u32[]{:S(2)}) collective-permute-start(bf16[256,256]{1,0:T(8,128)(2,1)S(1)} %pad_maximum_fusion.3), channel_id=1, source_target_pairs={{0,4},{1,5},{2,6},{3,7},{4,0},{5,1},{6,2},{7,3},{8,12},{9,13},{10,... | collective-permute-start | bytes 393224 | tf_op jit(solution)/shard_map/ppermute | solution.py:436
  111.0 4.7 %collective-permute-start.17 = (bf16[512,256]{1,0:T(8,128)(2,1)S(1)}, bf16[512,256]{1,0:T(8,128)(2,1)S(1)}, u32[]{:S(2)}, u32[]{:S(2)}) collective-permute-start(bf16[512,256]{1,0:T(8,128)(2,1)S(1)} %constant_dynamic-update-slice_fusion.3.refs_4_), channel_id=1, source_target_pairs={{0,1},{1,0},{2,3},{3,2},{4,5},{5,4},{6,7},{7,6},{8,9},{9,8},{10,11... | collective-permute-start | bytes 786440 | tf_op jit(solution)/shard_map/ppermute | solution.py:436
  113.0 19.3 %copy-start.1 = (bf16[512,512]{1,0:T(8,128)(2,1)S(1)}, bf16[512,512]{1,0:T(8,128)(2,1)}, u32[]{:S(2)}) copy-start(bf16[512,512]{1,0:T(8,128)(2,1)} %refs_4_.1) | copy-start | bytes 1572868
  113.0 8.7 %collective-permute-start.13 = (bf16[512,256]{1,0:T(8,128)(2,1)S(1)}, bf16[512,256]{1,0:T(8,128)(2,1)S(1)}, u32[]{:S(2)}, u32[]{:S(2)}) collective-permute-start(bf16[512,256]{1,0:T(8,128)(2,1)S(1)} %shard_map.143), channel_id=1, source_target_pairs={{0,8},{8,0},{16,24},{24,16},{1,9},{9,1},{17,25},{25,17},{2,10},{10... | collective-permute-start | bytes 786440 | tf_op jit(solution)/shard_map/ppermute | solution.py:436
  117.6 8.4 %collective-permute-start.18 = (bf16[512,256]{1,0:T(8,128)(2,1)S(1)}, bf16[512,256]{1,0:T(8,128)(2,1)S(1)}, u32[]{:S(2)}, u32[]{:S(2)}) collective-permute-start(bf16[512,256]{1,0:T(8,128)(2,1)S(1)} %shard_map.145), channel_id=1, source_target_pairs={{0,16},{8,24},{16,0},{24,8},{1,17},{9,25},{17,1},{25,9},{2,18},{10... | collective-permute-start | bytes 786440 | tf_op jit(solution)/shard_map/ppermute | solution.py:436
  126.1 5.0 %collective-permute-start.19 = (bf16[256,256]{1,0:T(8,128)(2,1)S(1)}, bf16[256,256]{1,0:T(8,128)(2,1)S(1)}, u32[]{:S(2)}, u32[]{:S(2)}) collective-permute-start(bf16[256,256]{1,0:T(8,128)(2,1)S(1)} %slice.74), channel_id=1, source_target_pairs={{0,8},{8,0},{16,24},{24,16},{1,9},{9,1},{17,25},{25,17},{2,10},{10... | collective-permute-start | bytes 393224 | tf_op jit(solution)/shard_map/ppermute | solution.py:436
  127.4 5.0 %collective-permute-start.14 = (bf16[256,256]{1,0:T(8,128)(2,1)S(1)}, bf16[256,256]{1,0:T(8,128)(2,1)S(1)}, u32[]{:S(2)}, u32[]{:S(2)}) collective-permute-start(bf16[256,256]{1,0:T(8,128)(2,1)S(1)} %slice.75), channel_id=1, source_target_pairs={{0,16},{8,24},{16,0},{24,8},{1,17},{9,25},{17,1},{25,9},{2,18},{10... | collective-permute-start | bytes 393224 | tf_op jit(solution)/shard_map/ppermute | solution.py:436
